TPU v7x, 32 devices: a whole 2x2x4 slice. The times are simulated.
32 devices in a mesh: narrow: 8 (over y, x, core), wide: 4 (over z).
Axes of the slice: x: 2, y: 2, z: 4, core: 2. Of those that a mesh axis runs over, the one named last changes fastest.
Arguments:
- feat_p2: float32 [4, 256, 64, 64], P('wide', 'narrow'), may hold values from -6 to 6
- feat_p3: float32 [4, 256, 32, 32], P('wide', 'narrow'), may hold values from -6 to 6
- feat_p4: float32 [4, 256, 16, 16], P('wide', 'narrow'), may hold values from -6 to 6
- feat_p5: float32 [4, 256, 8, 8], P('wide', 'narrow'), may hold values from -6 to 6
- rois: int32 [2, 4, 512, 4], P(None, 'wide'), may hold values from 0 to 256, as said below
- levels: int32 [2, 4, 512], P(None, 'wide'), may hold values from 0 to 3
- labels: int32 [2, 4, 512], P(None, 'wide'), may hold values from 0 to 80
- sampled: int32 [2, 4, 512], P(None, 'wide'), may hold values from 0 to 1
- targets: float32 [2, 4, 512, 4], P(None, 'wide'), may hold values from -6 to 6
- fc1_w: float32 [2, 12544, 1024], P(None, 'narrow'), may hold values from -0.078125 to 0.078125
- fc1_m: float32 [2, 12544, 1024], P(None, 'narrow'), may hold values from -0.09375 to 0.09375
- fc1_v: float32 [2, 12544, 1024], P(None, 'narrow'), may hold values from 2.4414063e-05 to 0.0001953125
- fc2_w: float32 [2, 1024, 1024], P(None, 'narrow'), may hold values from -0.1875 to 0.1875
- fc2_m: float32 [2, 1024, 1024], P(None, 'narrow'), may hold values from -0.09375 to 0.09375
- fc2_v: float32 [2, 1024, 1024], P(None, 'narrow'), may hold values from 2.4414063e-05 to 0.0001953125
- head_w: float32 [2, 1024, 401], P(None, 'narrow'), may hold values from -0.5 to 0.5
- head_m: float32 [2, 1024, 401], P(None, 'narrow'), may hold values from -0.09375 to 0.09375
- head_v: float32 [2, 1024, 401], P(None, 'narrow'), may hold values from 2.4414063e-05 to 0.0001953125
Outputs:
- loss_parts: float32 [2], replicated
- fc1_new: float32 [2, 12544, 1024], P(None, 'narrow')
- fc1_moment: float32 [2, 12544, 1024], P(None, 'narrow')
- fc1_second: float32 [2, 12544, 1024], P(None, 'narrow')
- fc2_new: float32 [2, 1024, 1024], P(None, 'narrow')
- fc2_moment: float32 [2, 1024, 1024], P(None, 'narrow')
- fc2_second: float32 [2, 1024, 1024], P(None, 'narrow')
- head_new: float32 [2, 1024, 401], P(None, 'narrow')
- head_moment: float32 [2, 1024, 401], P(None, 'narrow')
- head_second: float32 [2, 1024, 401], P(None, 'narrow')
Inputs may be any that keep to these rules, and one draw needn't show every extreme that they name: `rois`: integer boxes inside an image of 256 pixels, at least 4 cells wide on their level.
All inputs are finite; a program needn't handle non-finite values.
Results may differ from a plain program's by a relative error of at most 0.0008.
Values may be sent and summed in bfloat16 or wider, within the bound.
A program may use at most 448 MiB of HBM per device.

v0:
```python
from functools import partial

import jax
import jax.numpy as jnp
from jax import lax
from jax.sharding import PartitionSpec as P

CLASSES = 81
STEP = 5


BETA_ONE = 0.5
BETA_TWO = 0.5
RATE = 0.02
DECAY = 0.01
EPSILON = 1e-08
HIGH = lax.Precision.HIGHEST


def tent_rows(start, length, side):
    bins = jnp.arange(7, dtype=jnp.float32)
    offsets = jnp.array([0.25, 0.75], jnp.float32)
    where = (
        start[:, None, None]
        + (bins[None, :, None] + offsets[None, None, :]) * (length / 7.0)[:, None, None]
    )
    where = jnp.clip(where, 0.0, side - 1.0)
    cells = jnp.arange(side, dtype=jnp.float32)
    weight = jnp.maximum(0.0, 1.0 - jnp.abs(where[..., None] - cells))
    return jnp.mean(weight, axis=2)


def roi_pool(maps, boxes, levels):
    total = None
    corners = boxes.astype(jnp.float32)
    for level in range(4):
        fmap = maps[level]
        side = fmap.shape[1]
        scale = 1.0 / (4.0 * 2**level)
        pick = (levels == level).astype(jnp.float32)
        row_weights = (
            tent_rows(corners[:, 1] * scale - 0.5, (corners[:, 3] - corners[:, 1]) * scale, side)
            * pick[:, None, None]
        )
        col_weights = tent_rows(
            corners[:, 0] * scale - 0.5, (corners[:, 2] - corners[:, 0]) * scale, side
        )
        part = jnp.einsum("rih,chw->rciw", row_weights, fmap, precision=HIGH)
        part = jnp.einsum("rciw,rjw->rcij", part, col_weights, precision=HIGH)
        total = part if total is None else total + part
    return total.reshape(total.shape[0], -1)


def row_loss(logits, labels, sampled, targets):
    cls = logits[:, :CLASSES]
    box = logits[:, CLASSES:].reshape(logits.shape[0], CLASSES - 1, 4)
    top = jnp.max(cls, axis=1, keepdims=True)
    lse = top[:, 0] + jnp.log(jnp.sum(jnp.exp(cls - top), axis=1))
    onehot = (labels[:, None] == jnp.arange(CLASSES)[None, :]).astype(jnp.float32)
    picked = jnp.sum(cls * onehot, axis=1)
    weight = sampled.astype(jnp.float32)
    fore = onehot[:, 1:] * weight[:, None]
    chosen = jnp.einsum("rk,rkj->rj", fore, box, precision=HIGH)
    differ = chosen - targets * jnp.sum(fore, axis=1, keepdims=True)
    huber = jnp.where(jnp.abs(differ) < 1.0, 0.5 * differ * differ, jnp.abs(differ) - 0.5)
    return jnp.sum(weight * (lse - picked)) + jnp.sum(huber)


def silu_slope(value):
    sig = jax.nn.sigmoid(value)
    return sig * (1.0 + value * (1.0 - sig))


def inner_rows(left, right):
    return lax.dot_general(
        left, right, (((0,), (0,)), ((), ())), preferred_element_type=jnp.float32
    )


def adamw(weight, moment, second, grad):
    moment = BETA_ONE * moment + (1.0 - BETA_ONE) * grad
    second = BETA_TWO * second + (1.0 - BETA_TWO) * grad * grad
    fixed_m = moment / (1.0 - BETA_ONE**STEP)
    fixed_v = second / (1.0 - BETA_TWO**STEP)
    weight = weight - RATE * (fixed_m / (jnp.sqrt(fixed_v) + EPSILON) + DECAY * weight)
    return (weight, moment, second)


def pool_device(maps, boxes, levels):

    def one_image(items):
        fmaps, box, lev = items
        return roi_pool(fmaps, box, lev)

    pooled = lax.map(one_image, (maps, boxes, levels))
    return pooled.reshape(-1, pooled.shape[-1]).astype(jnp.bfloat16)


def own_rows(array, first, count):
    flat = array.reshape((-1,) + array.shape[2:])
    return lax.dynamic_slice_in_dim(flat, first, count, 0)


def per_device(
    feat_p2,
    feat_p3,
    feat_p4,
    feat_p5,
    rois,
    levels,
    labels,
    sampled,
    targets,
    fc1_w,
    fc1_m,
    fc1_v,
    fc2_w,
    fc2_m,
    fc2_v,
    head_w,
    head_m,
    head_v,
):
    maps = (feat_p2, feat_p3, feat_p4, feat_p5)
    rows_dev = rois.shape[1] * rois.shape[2]
    mine_rows = rows_dev // lax.axis_size("narrow")
    first = lax.axis_index("narrow") * mine_rows
    w1_low = fc1_w.astype(jnp.bfloat16)
    w2_full, wh_full = (
        lax.all_gather(fc2_w.astype(jnp.bfloat16), "narrow", axis=1, tiled=True),
        lax.all_gather(head_w.astype(jnp.bfloat16), "narrow", axis=1, tiled=True),
    )
    kept = []
    local_total = jnp.zeros((), jnp.float32)
    local_count = jnp.zeros((), jnp.float32)
    for index in range(2):
        pooled = pool_device(maps, rois[index], levels[index])

        def term(start, count, pooled=pooled, index=index):
            return jnp.dot(pooled, w1_low[index], preferred_element_type=jnp.float32)

        pre1 = lax.psum_scatter(
            term(jnp.int32(0), lax.axis_size("narrow") * mine_rows),
            "narrow",
            scatter_dimension=0,
            tiled=True,
        )
        hid1 = jax.nn.silu(pre1).astype(jnp.bfloat16)
        pre2 = jnp.dot(hid1, w2_full[index], preferred_element_type=jnp.float32)
        hid2 = jax.nn.silu(pre2).astype(jnp.bfloat16)
        logits = jnp.dot(hid2, wh_full[index], preferred_element_type=jnp.float32)
        lab = own_rows(labels[index], first, mine_rows)
        samp = own_rows(sampled[index], first, mine_rows)
        tgt = own_rows(targets[index], first, mine_rows)
        loss_fn = partial(row_loss, labels=lab, sampled=samp, targets=tgt)
        local_total = local_total + loss_fn(logits)
        local_count = local_count + jnp.sum(samp).astype(jnp.float32)
        kept.append((pooled, pre1, hid1, pre2, hid2, logits, loss_fn))
    total, count = lax.psum((local_total, local_count), ("narrow", "wide"))
    grads_one, grads_two, grads_head = ([], [], [])
    for index in range(2):
        pooled, pre1, hid1, pre2, hid2, logits, loss_fn = kept[index]
        _, pull = jax.vjp(loss_fn, logits)
        back_z = pull(jnp.ones((), jnp.float32) / count)[0].astype(jnp.bfloat16)
        grads_head.append(inner_rows(hid2, back_z))
        back_h2 = lax.dot_general(
            back_z, wh_full[index], (((1,), (1,)), ((), ())), preferred_element_type=jnp.float32
        )
        back_p2 = (back_h2 * silu_slope(pre2)).astype(jnp.bfloat16)
        grads_two.append(inner_rows(hid1, back_p2))
        back_h1 = lax.dot_general(
            back_p2, w2_full[index], (((1,), (1,)), ((), ())), preferred_element_type=jnp.float32
        )
        back_p1 = (back_h1 * silu_slope(pre1)).astype(jnp.bfloat16)
        back_all = lax.all_gather(back_p1, "narrow", axis=0, tiled=True)
        grads_one.append(inner_rows(pooled, back_all))
    grad_one = jnp.stack(grads_one)
    grad_two, grad_head = (
        lax.psum_scatter(jnp.stack(grads_two), "narrow", scatter_dimension=1, tiled=True),
        lax.psum_scatter(jnp.stack(grads_head), "narrow", scatter_dimension=1, tiled=True),
    )
    grad_one, grad_two, grad_head = lax.psum((grad_one, grad_two, grad_head), "wide")
    new1 = adamw(fc1_w, fc1_m, fc1_v, grad_one)
    new2 = adamw(fc2_w, fc2_m, fc2_v, grad_two)
    newh = adamw(head_w, head_m, head_v, grad_head)
    result = new1 + new2 + newh
    return (jnp.stack([total, count]),) + tuple(result)


def solution(mesh):
    return jax.shard_map(
        per_device,
        mesh=mesh,
        in_specs=(
            P("wide", "narrow", None, None),
            P("wide", "narrow", None, None),
            P("wide", "narrow", None, None),
            P("wide", "narrow", None, None),
            P(None, "wide", None, None),
            P(None, "wide", None),
            P(None, "wide", None),
            P(None, "wide", None),
            P(None, "wide", None, None),
            P(None, "narrow", None),
            P(None, "narrow", None),
            P(None, "narrow", None),
            P(None, "narrow", None),
            P(None, "narrow", None),
            P(None, "narrow", None),
            P(None, "narrow", None),
            P(None, "narrow", None),
            P(None, "narrow", None),
        ),
        out_specs=(
            P(),
            P(None, "narrow", None),
            P(None, "narrow", None),
            P(None, "narrow", None),
            P(None, "narrow", None),
            P(None, "narrow", None),
            P(None, "narrow", None),
            P(None, "narrow", None),
            P(None, "narrow", None),
            P(None, "narrow", None),
        ),
        check_vma=False,
    )
```

profile of v0, /device:TPU:0, one launch (start us, length us, event | category | flops | bytes accessed | tf_op | source)
XLA Modules:
  0.0 2177.1 jit_solution(3835627399578115614)
XLA Ops:
  7.2 1.9 convert_element_type.167
  11.9 2.0 copy.156
  15.6 26.9 %convolution_bitcast_fusion.1 = f32[512,32,7,64]{0,3,1,2:T(8,128)} fusion(f32[1,32,64,64]{3,2,1,0:T(8,128)S(1)} %copy-done, f32[512,7,64]{0,2,1:T(8,128)S(1)} %maximum_reduce_fusion.3, f32[512]{0:T(512)S(1)} %bitcast.261), kind=kOutput, calls=%fused_computation.8 | convolution fusion | flops 5637373952 | bytes 30803968 | tf_op jit(solution)/shard_map/while/body/eval_jaxpr/rih,chw->rciw/dot_general | solution.py:48
  42.5 51.9 %copy.116 = f32[512,32,7,64]{3,1,2,0:T(8,128)} copy(f32[512,32,7,64]{0,3,1,2:T(8,128)} %convolution_bitcast_fusion.1) | data formatting | bytes 58720256 | tf_op jit(solution)/shard_map/while/body/eval_jaxpr/rih,chw->rciw/transpose | solution.py:48
  94.6 16.7 convolution_bitcast_fusion.3
  111.3 44.4 %copy.119 = f32[512,32,7,32]{3,1,2,0:T(8,128)} copy(f32[512,32,7,32]{0,3,1,2:T(8,128)} %convolution_bitcast_fusion.3) | data formatting | bytes 29360128 | tf_op jit(solution)/shard_map/while/body/eval_jaxpr/rih,chw->rciw/transpose | solution.py:48
  155.9 1.9 copy.159
  158.0 8.0 convolution_bitcast_fusion.7
  166.0 20.5 copy.122
  187.4 5.4 convolution_bitcast_fusion.11
  192.8 9.6 copy.125
  202.5 2.0 copy.163
  204.5 222.6 %fusion.100 = f32[512,32,7,7]{1,3,2,0:T(8,128)} fusion(f32[512,32,7,64]{3,1,2,0:T(8,128)} %copy.116, f32[512,7,64,1]{2,1,3,0:T(8,128)} %copy.156), kind=kOutput, calls=%fused_computation.279 | convolution fusion | flops 616562688 | bytes 33488896 | tf_op jit(solution)/shard_map/while/body/eval_jaxpr/rciw,rjw->rcij/dot_general | solution.py:49
  427.1 213.0 %fusion.101 = f32[512,32,7,7]{1,3,2,0:T(8,128)} fusion(f32[512,32,7,32]{3,1,2,0:T(8,128)} %copy.119, f32[512,7,32,1]{2,1,3,0:T(8,128)S(1)} %copy-done.3), kind=kOutput, calls=%fused_computation.280 | convolution fusion | flops 308281344 | bytes 18350080 | tf_op jit(solution)/shard_map/while/body/eval_jaxpr/rciw,rjw->rcij/dot_general | solution.py:49
  640.1 22.8 %fusion.102 = f32[512,32,7,7]{1,3,2,0:T(8,128)} fusion(f32[512,32,7,16]{1,3,2,0:T(8,128)} %copy.122, f32[512,7,16,1]{2,1,3,0:T(8,128)S(1)} %copy.161), kind=kOutput, calls=%fused_computation.281 | convolution fusion | flops 154140672 | bytes 10780672 | tf_op jit(solution)/shard_map/while/body/eval_jaxpr/rciw,rjw->rcij/dot_general | solution.py:49
  662.9 28.1 %add_convert_fusion.1 = bf16[512,32,7,7]{1,3,2,0:T(8,128)(2,1)} fusion(f32[512,32,7,7]{1,3,2,0:T(8,128)} %fusion.102, f32[512,32,7,7]{1,3,2,0:T(8,128)} %fusion.100, f32[512,32,7,7]{1,3,2,0:T(8,128)} %fusion.101, f32[512,32,7,8]{1,3,2,0:T(8,128)} %copy.125, f32[512,7,8,1]{2,1,3,0:T(8,128)} %copy.163), kind=kOutput, calls=%fused_computation.3 | convolution fusion | flops 80281600 | bytes 15024128 | tf_op jit(solution)/shard_map/while/body/eval_jaxpr/rciw,rjw->rcij/dot_general | solution.py:49
  691.0 8.5 copy.127
  699.6 1.8 convert_element_type.162
  701.4 8.4 convert_element_type.163
  709.8 5.9 fusion.2
  719.2 27.0 %convolution_bitcast_fusion = f32[512,32,7,64]{0,3,1,2:T(8,128)} fusion(f32[1,32,64,64]{3,2,1,0:T(8,128)S(1)} %copy-done, f32[512,7,64]{0,2,1:T(8,128)S(1)} %maximum_reduce_fusion.1, f32[512]{0:T(512)S(1)} %bitcast.260), kind=kOutput, calls=%fused_computation.7 | convolution fusion | flops 5637373952 | bytes 30803968 | tf_op jit(solution)/shard_map/while/body/eval_jaxpr/rih,chw->rciw/dot_general | solution.py:48
  746.1 51.9 %copy.130 = f32[512,32,7,64]{3,1,2,0:T(8,128)} copy(f32[512,32,7,64]{0,3,1,2:T(8,128)} %convolution_bitcast_fusion) | data formatting | bytes 58720256 | tf_op jit(solution)/shard_map/while/body/eval_jaxpr/rih,chw->rciw/transpose | solution.py:48
  798.5 2.0 copy.171
  800.7 16.6 convolution_bitcast_fusion.2
  817.3 44.5 %copy.133 = f32[512,32,7,32]{3,1,2,0:T(8,128)} copy(f32[512,32,7,32]{0,3,1,2:T(8,128)} %convolution_bitcast_fusion.2) | data formatting | bytes 29360128 | tf_op jit(solution)/shard_map/while/body/eval_jaxpr/rih,chw->rciw/transpose | solution.py:48
  861.9 1.9 copy.174
  864.0 8.0 convolution_bitcast_fusion.6
  872.0 20.5 copy.136
  893.5 1.9 copy.178
  895.5 5.4 convolution_bitcast_fusion.10
  900.9 9.6 copy.139
  910.5 213.0 %fusion.103 = f32[512,32,7,7]{1,3,2,0:T(8,128)} fusion(f32[512,32,7,64]{3,1,2,0:T(8,128)} %copy.130, f32[512,7,64,1]{2,1,3,0:T(8,128)} %copy.171), kind=kOutput, calls=%fused_computation.282 | convolution fusion | flops 616562688 | bytes 33488896 | tf_op jit(solution)/shard_map/while/body/eval_jaxpr/rciw,rjw->rcij/dot_general | solution.py:49
  1123.5 23.1 %fusion.105 = f32[512,32,7,7]{1,3,2,0:T(8,128)} fusion(f32[512,32,7,16]{1,3,2,0:T(8,128)} %copy.136, f32[512,7,16,1]{2,1,3,0:T(8,128)S(1)} %copy.176), kind=kOutput, calls=%fused_computation.284 | convolution fusion | flops 154140672 | bytes 10780672 | tf_op jit(solution)/shard_map/while/body/eval_jaxpr/rciw,rjw->rcij/dot_general | solution.py:49
  1146.6 213.0 %fusion.104 = f32[512,32,7,7]{1,3,2,0:T(8,128)} fusion(f32[512,32,7,32]{3,1,2,0:T(8,128)} %copy.133, f32[512,7,32,1]{2,1,3,0:T(8,128)S(1)} %copy-done.2), kind=kOutput, calls=%fused_computation.283 | convolution fusion | flops 308281344 | bytes 18350080 | tf_op jit(solution)/shard_map/while/body/eval_jaxpr/rciw,rjw->rcij/dot_general | solution.py:49
  1359.6 27.8 %add_convert_fusion = bf16[512,32,7,7]{1,3,2,0:T(8,128)(2,1)} fusion(f32[512,32,7,7]{1,3,2,0:T(8,128)} %fusion.105, f32[512,32,7,7]{1,3,2,0:T(8,128)} %fusion.103, f32[512,32,7,7]{1,3,2,0:T(8,128)} %fusion.104, f32[512,32,7,8]{1,3,2,0:T(8,128)} %copy.139, f32[512,7,8,1]{2,1,3,0:T(8,128)S(1)} %copy-done.4), kind=kOutput, calls=%fused_computation.2 | convolution fusion | flops 80281600 | bytes 15024128 | tf_op jit(solution)/shard_map/while/body/eval_jaxpr/rciw,rjw->rcij/dot_general | solution.py:49
  1387.4 8.5 copy.141
  1396.0 1.5 convert_element_type.173
  1397.5 5.8 fusion.1
  1403.3 42.2 %psum.36 = f32[]{:T(128)} all-reduce(f32[]{:T(128)S(6)} %add.962), channel_id=1, replica_groups=mesh['narrow'=8,'wide'=4] {'narrow','wide'}, use_global_device_ids=true, to_apply=%region_33.34 | all-reduce | flops 1 | bytes 8 | tf_op jit(solution)/shard_map/psum | solution.py:159
  1448.5 5.6 fusion.96
  1454.1 2.2 fusion.4
  1456.3 1.8 fusion.24
  1459.8 2.2 fusion.6
  1463.3 1.8 fusion.11
  1465.2 3.1 fusion.9
  1471.0 3.0 fusion.10
  1475.2 2.0 pad_maximum_fusion.2
  1478.8 4.2 pad_maximum_fusion.1
  1483.3 8.7 all-gather.9.cloned.1.call-done
  1492.0 5.8 convolution_bitcast_fusion.5
  1497.8 20.1 all-gather.11.cloned.1.call-done
  1517.9 6.3 convolution_bitcast_fusion.4
  1524.2 12.8 pad_maximum_fusion
  1537.0 31.7 %reduce-scatter.11.cloned.1.call-done = f32[2,128,401]{1,2,0:T(8,128)} async-done(((f32[2,1024,401]{1,2,0:T(8,128)}), f32[2,128,401]{1,2,0:T(8,128)}) %reduce-scatter.11.cloned.1.call-update) | async-done | bytes 410640 | tf_op jit(solution)/shard_map/reduce_scatter | solution.py:180
  1568.7 75.3 %reduce-scatter.9.cloned.1.call-done = f32[2,128,1024]{2,1,0:T(8,128)} async-done(((f32[2,1024,1024]{2,1,0:T(8,128)}), f32[2,128,1024]{2,1,0:T(8,128)}) %reduce-scatter.9.cloned.1.call-update) | async-done | bytes 1048592 | tf_op jit(solution)/shard_map/reduce_scatter | solution.py:179
  1646.6 49.5 %psum.35 = f32[1]{0:T(128)} all-reduce(f32[1]{0:T(128)} %bitcast.98), channel_id=1, replica_groups=mesh['narrow'=8,'wide'=4] {'narrow','wide'}, use_global_device_ids=true, to_apply=%region_30.31 | all-reduce | flops 1 | bytes 8 | tf_op jit(solution)/shard_map/psum | solution.py:159
  1696.1 1.9 pad_maximum_fusion.3
  1698.0 434.4 %all-reduce.7.cloned.1.call-done = (f32[2,1568,1024]{2,1,0:T(8,128)}, f32[2,128,1024]{2,1,0:T(8,128)}, f32[2,128,401]{1,2,0:T(8,128)}) async-done(((f32[2,1568,1024]{2,1,0:T(8,128)}, f32[2,128,1024]{2,1,0:T(8,128)}, f32[2,128,401]{1,2,0:T(8,128)}), (f32[2,1568,1024]{2,1,0:T(8,128)}, f32[2,128,1024]{2,1,0:T(8,128)}, f32[2,128,401]{1,2,0:T(8,128)})) %all-reduce.7.cloned.1.call-update) | async-done | bytes 14304272 | tf_op jit(solution)/shard_map/psum | solution.py:182
  2132.4 1.3 multiply_subtract_fusion.2
  2133.7 1.0 copy.151
  2134.7 1.0 copy.152
  2135.6 1.0 copy.153
  2136.6 31.5 %multiply_subtract_fusion = (f32[2,1568,1024]{2,1,0:T(8,128)}, f32[2,1568,1024]{2,1,0:T(8,128)}, f32[2,1568,1024]{2,1,0:T(8,128)}) fusion(f32[2,1568,1024]{2,1,0:T(8,128)} %param.43, f32[2,1568,1024]{2,1,0:T(8,128)} %get-tuple-element.150, f32[2,1568,1024]{2,1,0:T(8,128)} %param.44, f32[2,1568,1024]{2,1,0:T(8,128)} %param.45), kind=kLoop, calls=%fused_computation.6 | loop fusion | flops 44957696 | bytes 89915392 | tf_op jit(solution)/shard_map/sub | solution.py:85
  2168.1 2.2 multiply_subtract_fusion.1
  (186 shorter events, 20.7 us)
Async XLA Ops:
  7.2 8.4 copy-start
  7.2 7.8 copy-start.39
  7.2 1441.3 %all-gather.7.cloned.1.call-start = ((), (), s32[]{:S(2)}) async-start(), calls=%async_computation.6 | async-start | bytes 1847808 | tf_op jit(solution)/shard_map/all_gather | solution.py:131
  9.2 1444.9 %reduce-scatter.5.cloned.1.call-start = ((), (), s32[]{:S(2)}) async-start(), calls=%async_computation.4 | async-start | bytes 2359296 | tf_op jit(solution)/shard_map/reduce_scatter | solution.py:142
  42.5 52.0 %copy-start.7 = (f32[1,32,32,32]{3,2,1,0:T(8,128)S(1)}, f32[1,32,32,32]{3,2,1,0:T(8,128)}, u32[]{:S(2)}) copy-start(f32[1,32,32,32]{3,2,1,0:T(8,128)} %param.35) | copy-start | bytes 393220
  155.7 2.3 copy-start.14
  166.0 21.4 copy-start.20
  204.5 222.6 %copy-start.3 = (f32[512,7,32,1]{2,1,3,0:T(8,128)S(1)}, f32[512,7,32,1]{2,1,3,0:T(8,128)}, u32[]{:S(2)}) copy-start(f32[512,7,32,1]{2,1,3,0:T(8,128)} %copy.159) | copy-start | bytes 1376260
  709.8 6.0 copy-start.5
  715.7 1.0 copy-start.40
  715.7 3.1 copy-start.30
  715.7 3.4 copy-start.32
  715.7 738.4 %all-gather.5.cloned.1.call-start = ((), (), s32[]{:S(2)}) async-start(), calls=%async_computation.5 | async-start | bytes 4718592 | tf_op jit(solution)/shard_map/all_gather | solution.py:130
  716.7 743.1 %reduce-scatter.7.cloned.1.call-start = ((), (), s32[]{:S(2)}) async-start(), calls=%async_computation.7 | async-start | bytes 2359296 | tf_op jit(solution)/shard_map/reduce_scatter | solution.py:142
  716.8 29.3 %copy-start.37 = (s32[1,1,512]{2,1,0:T(1,128)}, s32[1,1,512]{2,1,0:T(1,128)S(1)}, u32[]{:S(2)}) copy-start(s32[1,1,512]{2,1,0:T(1,128)S(1)} %get-tuple-element.246) | copy-start | bytes 6148
  716.8 29.3 %copy-start.38 = (s32[1,1,512]{2,1,0:T(1,128)}, s32[1,1,512]{2,1,0:T(1,128)S(1)}, u32[]{:S(2)}) copy-start(s32[1,1,512]{2,1,0:T(1,128)S(1)} %get-tuple-element.247) | copy-start | bytes 6148
  746.1 51.9 %copy-start.31 = (f32[512,7,2]{0,2,1:T(2,128)S(1)}, f32[512,7,2]{0,2,1:T(2,128)}, u32[]{:S(2)}) copy-start(f32[512,7,2]{0,2,1:T(2,128)} %get-tuple-element.240) | copy-start | bytes 86020
  798.0 2.4 copy-start.29
  798.0 2.6 copy-start.8
  798.0 2.6 copy-start.36
  817.3 44.5 %copy-start.28 = (f32[512,7,2]{0,2,1:T(2,128)S(1)}, f32[512,7,2]{0,2,1:T(2,128)}, u32[]{:S(2)}) copy-start(f32[512,7,2]{0,2,1:T(2,128)} %get-tuple-element.242) | copy-start | bytes 86020
  817.3 46.6 %copy-start.27 = (f32[512,7,2]{0,2,1:T(2,128)S(1)}, f32[512,7,2]{0,2,1:T(2,128)}, u32[]{:S(2)}) copy-start(f32[512,7,2]{0,2,1:T(2,128)} %get-tuple-element.243) | copy-start | bytes 86020
  861.7 2.3 copy-start.15
  861.7 2.3 copy-start.35
  872.0 20.5 copy-start.26
  872.0 21.4 copy-start.24
  892.5 2.9 copy-start.25
  892.5 2.9 copy-start.21
  892.5 2.9 copy-start.34
  1123.5 23.1 %copy-start.2 = (f32[512,7,32,1]{2,1,3,0:T(8,128)S(1)}, f32[512,7,32,1]{2,1,3,0:T(8,128)}, u32[]{:S(2)}) copy-start(f32[512,7,32,1]{2,1,3,0:T(8,128)} %copy.174) | copy-start | bytes 1376260
  1146.6 213.0 %copy-start.4 = (f32[512,7,8,1]{2,1,3,0:T(8,128)S(1)}, f32[512,7,8,1]{2,1,3,0:T(8,128)}, u32[]{:S(2)}) copy-start(f32[512,7,8,1]{2,1,3,0:T(8,128)} %copy.178) | copy-start | bytes 344068
  1397.5 50.1 %copy-start.41 = (s32[2,1,512]{2,1,0:T(1,128)S(1)}, s32[2,1,512]{2,1,0:T(1,128)}, u32[]{:S(2)}) copy-start(s32[2,1,512]{2,1,0:T(1,128)} %param.40) | copy-start | bytes 12292
  1397.5 51.0 %copy-start.33 = (f32[2,1,512,4]{2,3,1,0:T(4,128)S(1)}, f32[2,1,512,4]{2,3,1,0:T(4,128)}, u32[]{:S(2)}) copy-start(f32[2,1,512,4]{2,3,1,0:T(4,128)} %param.42) | copy-start | bytes 49156
  1403.3 88.7 %all-gather.9.cloned.1.call-start = ((), (), s32[]{:S(2)}) async-start(), calls=%async_computation.8 | async-start | bytes 1179648 | tf_op jit(solution)/shard_map/all_gather | solution.py:175
  1459.8 5.4 copy-start.18
  1465.2 4.0 copy-start.22
  1465.2 5.8 copy-start.19
  1468.3 49.6 %all-gather.11.cloned.1.call-start = ((), (), s32[]{:S(2)}) async-start(), calls=%async_computation.9 | async-start | bytes 1179648 | tf_op jit(solution)/shard_map/all_gather | solution.py:175
  1474.0 94.7 %reduce-scatter.11.cloned.1.call-start = ((), (), s32[]{:S(2)}) async-start(), calls=%async_computation.11 | async-start | bytes 3760128 | tf_op jit(solution)/shard_map/reduce_scatter | solution.py:180
  1475.1 2.1 copy-start.23
  1477.2 166.8 %reduce-scatter.9.cloned.1.call-start = ((), (), s32[]{:S(2)}) async-start(), calls=%async_computation.10 | async-start | bytes 9437184 | tf_op jit(solution)/shard_map/reduce_scatter | solution.py:179
  1483.0 9.0 copy-start.10
  1483.1 649.3 %all-reduce.7.cloned.1.call-start = ((), (), s32[]{:S(2)}) async-start(), calls=%async_computation.12 | async-start | bytes 28622848 | tf_op jit(solution)/shard_map/psum | solution.py:182
  1644.0 488.4 %copy-start.9 = (f32[2,128,401]{1,0,2:T(2,128)S(1)}, f32[2,128,401]{1,0,2:T(2,128)}, u32[]{:S(2)}) copy-start(f32[2,128,401]{1,0,2:T(2,128)} %param.49) | copy-start | bytes 1231876
  1644.0 488.4 %copy-start.16 = (f32[2,128,401]{1,0,2:T(2,128)S(1)}, f32[2,128,401]{1,0,2:T(2,128)}, u32[]{:S(2)}) copy-start(f32[2,128,401]{1,0,2:T(2,128)} %param.50) | copy-start | bytes 1231876
  1644.0 488.4 %copy-start.17 = (f32[2,128,401]{1,0,2:T(2,128)S(1)}, f32[2,128,401]{1,0,2:T(2,128)}, u32[]{:S(2)}) copy-start(f32[2,128,401]{1,0,2:T(2,128)} %param.51) | copy-start | bytes 1231876
  2136.6 31.5 %copy-start.6 = (f32[2,128,1024]{2,1,0:T(8,128)S(1)}, f32[2,128,1024]{2,1,0:T(8,128)}, u32[]{:S(2)}) copy-start(f32[2,128,1024]{2,1,0:T(8,128)} %param.46) | copy-start | bytes 3145732
  2136.6 31.5 %copy-start.11 = (f32[2,128,1024]{2,1,0:T(8,128)S(1)}, f32[2,128,1024]{2,1,0:T(8,128)}, u32[]{:S(2)}) copy-start(f32[2,128,1024]{2,1,0:T(8,128)} %param.47) | copy-start | bytes 3145732
  2136.6 31.5 %copy-start.12 = (f32[2,128,1024]{2,1,0:T(8,128)S(1)}, f32[2,128,1024]{2,1,0:T(8,128)}, u32[]{:S(2)}) copy-start(f32[2,128,1024]{2,1,0:T(8,128)} %param.48) | copy-start | bytes 3145732
  2136.6 31.5 %copy-start.13 = (f32[2,128,1024]{2,1,0:T(8,128)S(1)}, f32[2,128,1024]{2,1,0:T(8,128)}, u32[]{:S(2)}) copy-start(f32[2,128,1024]{2,1,0:T(8,128)} %get-tuple-element.151) | copy-start | bytes 3145732
  2136.6 33.8 %copy-start.1 = (f32[1,32,64,64]{3,2,1,0:T(8,128)S(1)}, f32[1,32,64,64]{3,2,1,0:T(8,128)}, u32[]{:S(2)}) copy-start(f32[1,32,64,64]{3,2,1,0:T(8,128)} %param.34) | copy-start | bytes 1572868
Sparse Core Ops, SparseCore 0:
  10.5 35.8 all-gather.6
  715.9 43.8 reduce-scatter.4
  762.4 36.6 all-gather.4
  1403.4 44.3 reduce-scatter.6
  1468.4 23.5 all-gather.8
  1494.4 23.4 all-gather.10
  1521.3 47.3 reduce-scatter.10
  1572.7 71.2 reduce-scatter.8
  1647.6 484.7 all-reduce.6
where the time goes:
time: 2180 us
  matrix products  1120 us (51%)
  waiting for transfers between devices  570 us (26%)
  local copies, waits for them, and re-layouts  296 us (14%)
  blocking collectives  91.7 us (4%)
  other arithmetic  80.3 us (4%)
    dot_general x8, matrix products, roi_pool(): part = jnp.einsum('rciw,rjw->rcij', part, col_weights, precision=HIGH)  963 us
    psum x1, waiting for transfers between devices, per_device(): lax.psum((grad_one, grad_two, grad_head), 'wide')  434 us
    transpose x8, local copies, waits for them, and re-layouts, roi_pool(): part = jnp.einsum('rih,chw->rciw', row_weights, fmap, precision=HIGH)  253 us
    dot_general x8, matrix products, roi_pool(): part = jnp.einsum('rih,chw->rciw', row_weights, fmap, precision=HIGH)  114 us
    psum x2, blocking collectives, per_device(): total, count = lax.psum((local_total, local_count), ('narrow', 'wide'))  91.7 us
    reduce_scatter x1, waiting for transfers between devices, per_device(): lax.psum_scatter(jnp.stack(grads_two), 'narrow', scatter_dimension=1, til...  75.3 us
  transfers between devices with their start and end apart: 9, of which 5 were waited for; matrix products, arithmetic and copies ran while one was open for 66% of the time, Pallas kernels for 0%

commit v1 on v0

v1 whole, which is shorter than its diff:
```python
from functools import partial

import jax
import jax.numpy as jnp
from jax import lax
from jax.experimental import pallas as pl
from jax.experimental.pallas import tpu as pltpu
from jax.sharding import PartitionSpec as P

CLASSES = 81
STEP = 5
BETA_ONE = 0.5
BETA_TWO = 0.5
RATE = 0.02
DECAY = 0.01
EPSILON = 1e-08
BINS = 7
CHUNK = 8
LANES = 128
MIB = 2**20


def tent(where, cells):
    return 0.5 * sum(jnp.maximum(0.0, 1.0 - jnp.abs(w - cells)) for w in where)


def pool_kernel(channels, side, span_ref, feat_ref, param_ref, out_ref, cols_ref, rows_ref, acc_ref, line_ref):
    step_id = pl.program_id(0)
    half = LANES // 2
    for group in range(2):
        y_start, y_step, top, base, x_start, x_step = (
            param_ref[group, k : k + 1, :] for k in range(6)
        )
        cells = lax.broadcasted_iota(jnp.int32, (side, LANES), 0).astype(jnp.float32)
        for j in range(BINS):
            where = [jnp.clip(x_start + (j + off) * x_step, 0.0, top) for off in (0.25, 0.75)]
            weight = tent(where, cells)
            high = weight.astype(jnp.bfloat16)
            low = (weight - high.astype(jnp.float32)).astype(jnp.bfloat16)
            lanes = pl.ds(j * LANES, LANES)
            cols_ref[0:side, lanes] = high
            cols_ref[side : 2 * side, lanes] = high
            cols_ref[2 * side : 3 * side, lanes] = low
            cols_ref[3 * side : 4 * side, lanes] = low
        acc_ref[...] = jnp.zeros_like(acc_ref)
        bins = lax.broadcasted_iota(jnp.int32, (8, LANES), 0).astype(jnp.float32)
        y_where = [jnp.clip(y_start + (bins + off) * y_step, 0.0, top) for off in (0.25, 0.75)]
        first = span_ref[(step_id * 2 + group) * 2]
        chunks = span_ref[(step_id * 2 + group) * 2 + 1]

        @pl.loop(0, chunks)
        def _(t):
            row = first + t * CHUNK
            for h in range(CHUNK):
                rows_ref[h] = tent(y_where, (row + h).astype(jnp.float32) - base)
            left = feat_ref[0, pl.ds(pl.multiple_of(row * channels, channels), CHUNK * channels), :]
            left = jnp.concatenate([left, left], axis=1)
            for j0 in range(0, BINS, 2):
                width = min(2, BINS - j0)
                part = jnp.dot(
                    left,
                    cols_ref[:, j0 * LANES : (j0 + width) * LANES],
                    preferred_element_type=jnp.float32,
                )
                for j in range(j0, j0 + width):
                    mine = part[:, (j - j0) * LANES : (j - j0 + 1) * LANES]
                    for i in range(BINS):
                        total = acc_ref[i * BINS + j]
                        for h in range(CHUNK):
                            total = total + rows_ref[h, i : i + 1, :] * mine[h * channels : (h + 1) * channels]
                        acc_ref[i * BINS + j] = total

        for ij in range(BINS * BINS):
            line_ref[group, pl.ds(ij, channels, stride=BINS * BINS), :] = acc_ref[ij]
    a, b = line_ref[0], line_ref[1]
    lanes = lax.broadcasted_iota(jnp.int32, a.shape, 1)
    out_ref[0] = jnp.where(lanes < half, a, pltpu.roll(b, half, 1)).astype(jnp.bfloat16)
    out_ref[1] = jnp.where(lanes < half, pltpu.roll(a, half, 1), b).astype(jnp.bfloat16)


def pool(feat, table, spans, shift, images, channels):
    total, height, depth = feat.shape
    blocks = table.shape[1]
    wide = channels * BINS * BINS
    side = depth // 2

    def kernel(order_ref, span_ref, *refs):
        pool_kernel(channels, side, span_ref, *refs)

    order = lax.rem(shift + jnp.arange(images, dtype=jnp.int32), total)
    spans = jnp.take(spans.reshape(total, -1), order, axis=0).reshape(-1)
    steps = images * blocks
    return pl.pallas_call(
        kernel,
        out_shape=jax.ShapeDtypeStruct((2, wide, steps * LANES), jnp.bfloat16),
        grid_spec=pltpu.PrefetchScalarGridSpec(
            num_scalar_prefetch=2,
            grid=(steps,),
            in_specs=[
                pl.BlockSpec((1, height, depth), lambda s, order, spans: (order[s // blocks], 0, 0)),
                pl.BlockSpec(
                    (None, None, 2, 8, LANES),
                    lambda s, order, spans: (order[s // blocks], lax.rem(s, blocks), 0, 0, 0),
                ),
            ],
            out_specs=pl.BlockSpec((2, wide, LANES), lambda s, order, spans: (0, 0, s)),
            scratch_shapes=[
                pltpu.VMEM((2 * depth, BINS * LANES), jnp.bfloat16),
                pltpu.VMEM((CHUNK, 8, LANES), jnp.float32),
                pltpu.VMEM((BINS * BINS, channels, LANES), jnp.float32),
                pltpu.VMEM((2, wide, LANES), jnp.float32),
            ],
        ),
        compiler_params=pltpu.CompilerParams(vmem_limit_bytes=40 * MIB),
        cost_estimate=pl.CostEstimate(
            flops=steps * 2 * 30 * channels * BINS * LANES * 4 * depth,
            bytes_accessed=steps * wide * LANES * 4,
            transcendentals=0,
        ),
        name="pool_rois",
    )(order, spans, feat, table)


def feature_rows(maps):
    side = maps[0].shape[-1]
    parts = [
        jnp.pad(m.transpose(0, 2, 1, 3), ((0, 0), (0, 0), (0, 0), (0, side - m.shape[-1])))
        for m in maps
    ]
    full = jnp.concatenate(parts, axis=1)
    high = lax.reduce_precision(full, 8, 7)
    low = (full - high).astype(jnp.bfloat16)
    full = jnp.concatenate([high.astype(jnp.bfloat16), low], axis=-1)
    return full.reshape(full.shape[0], -1, 2 * side)


def box_order(boxes, levels, side):
    base = 2 * side - 2 * (side >> levels)
    key = ((boxes[..., 1] + boxes[..., 3]) >> levels) + base * 8
    key = key * key.shape[-1] + jnp.arange(key.shape[-1], dtype=jnp.int32)
    return jnp.sum((key[..., :, None] > key[..., None, :]).astype(jnp.int32), axis=-1)


def box_table(boxes, levels, rank, side):
    count = boxes.shape[1]
    hot = (rank[:, None, :] == jnp.arange(count, dtype=jnp.int32)[:, None]).astype(jnp.bfloat16)
    both = jnp.concatenate([boxes, levels[..., None]], axis=-1).astype(jnp.bfloat16)
    both = jnp.einsum("psr,prk->kps", hot, both, preferred_element_type=jnp.float32)
    level = both[4]
    scale = jnp.where(level < 0.5, 0.25, jnp.where(level < 1.5, 0.125, jnp.where(level < 2.5, 0.0625, 0.03125)))
    height = scale * (4 * side)
    base = 2.0 * side - 2.0 * height
    top = height - 1.0
    rows = sum(side >> k for k in range(4))

    def axis(low, high):
        return low * scale - 0.5, ((high - low) * scale) / 7.0

    x_start, x_step = axis(both[0], both[2])
    y_start, y_step = axis(both[1], both[3])
    low = base + jnp.floor(jnp.clip(y_start, 0.0, top))
    high = base + jnp.floor(jnp.clip(y_start + 7.0 * y_step, 0.0, top)) + 1.0
    half = LANES // 2

    def split(v):
        return v.reshape(2, count // half, half)

    low = jnp.min(split(low), axis=(0, 2), keepdims=True)
    high = jnp.minimum(jnp.max(split(high), axis=(0, 2), keepdims=True), rows - 1.0)
    chunks = jnp.floor((high - low + CHUNK) / CHUNK)
    first = jnp.maximum(jnp.minimum(low, rows - chunks * CHUNK), 0.0)
    parts = [split(v) for v in (y_start, y_step, top, base, x_start, x_step)]
    parts += [jnp.broadcast_to(v, parts[0].shape) for v in (first, chunks)]
    return jnp.stack(parts).transpose(2, 0, 1, 3).reshape(count // LANES, 2, 8, LANES)


def adamw(weight, moment, second, grad):
    moment = BETA_ONE * moment + (1.0 - BETA_ONE) * grad
    second = BETA_TWO * second + (1.0 - BETA_TWO) * grad * grad
    fixed_m = moment / (1.0 - BETA_ONE**STEP)
    fixed_v = second / (1.0 - BETA_TWO**STEP)
    weight = weight - RATE * (fixed_m / (jnp.sqrt(fixed_v) + EPSILON) + DECAY * weight)
    return (weight, moment, second)


def update_kernel(images, boxes, me_ref, own_ref, other_ref, back_ref, w_ref, m_ref, v_ref, *outs):
    me = me_ref[0]

    def rows(k):
        image = lax.rem(me + k, images)
        return back_ref[pl.ds(pl.multiple_of(image * boxes, boxes), boxes), :]

    grad = jnp.dot(own_ref[...], rows(0), preferred_element_type=jnp.float32)
    for k in range(1, images):
        grad += jnp.dot(
            other_ref[:, (k - 1) * boxes : k * boxes], rows(k), preferred_element_type=jnp.float32
        )
    new = adamw(w_ref[...], m_ref[...], v_ref[...], grad)
    for ref, value in zip(outs, new):
        ref[...] = value


def update_first(me, own, other, back, weight, moment, second):
    passes, wide, hidden = weight.shape
    boxes = own.shape[2]
    images = back.shape[1] // boxes
    block = wide // BINS
    big = pl.BlockSpec((None, block, hidden), lambda p, b, me: (p, b, 0))
    return pl.pallas_call(
        partial(update_kernel, images, boxes),
        out_shape=[jax.ShapeDtypeStruct(weight.shape, jnp.float32)] * 3,
        grid_spec=pltpu.PrefetchScalarGridSpec(
            num_scalar_prefetch=1,
            grid=(passes, BINS),
            in_specs=[
                pl.BlockSpec((None, block, boxes), lambda p, b, me: (p, b, 0)),
                pl.BlockSpec((None, block, (images - 1) * boxes), lambda p, b, me: (p, b, 0)),
                pl.BlockSpec(
                    (None, images * boxes, hidden), lambda p, b, me: (p, 0, 0), pipeline_mode=pl.Buffered(1)
                ),
                big,
                big,
                big,
            ],
            out_specs=[big] * 3,
        ),
        compiler_params=pltpu.CompilerParams(vmem_limit_bytes=56 * MIB),
        cost_estimate=pl.CostEstimate(
            flops=2 * passes * wide * hidden * images * boxes,
            bytes_accessed=passes * wide * hidden * 24 + passes * images * boxes * (wide + hidden) * 2,
            transcendentals=passes * wide * hidden,
        ),
        name="update_first",
    )(me, own, other, back, weight, moment, second)


def silu_slope(value):
    sig = jax.nn.sigmoid(value)
    return sig * (1.0 + value * (1.0 - sig))


def loss_and_slope(logits, labels, sampled, targets, count):
    place = lax.broadcasted_iota(jnp.int32, logits.shape, 1)
    is_class = place < CLASSES
    weight = sampled.astype(jnp.float32)[:, None]
    label = labels[:, None]
    top = jnp.max(jnp.where(is_class, logits, -jnp.inf), axis=1, keepdims=True)
    grown = jnp.where(is_class, jnp.exp(jnp.where(is_class, logits - top, 0.0)), 0.0)
    norm = jnp.sum(grown, axis=1, keepdims=True)
    hot = place == label
    picked = jnp.sum(jnp.where(hot, logits, 0.0), axis=1, keepdims=True)
    fore = jnp.where(label > 0, weight, 0.0)
    total = jnp.sum(weight * (top + jnp.log(norm) - picked))
    slope = weight * (grown / norm - hot.astype(jnp.float32))
    for k in range(4):
        mask = place == CLASSES + 4 * (label - 1) + k
        mask = mask & (label > 0)
        chosen = fore * jnp.sum(jnp.where(mask, logits, 0.0), axis=1, keepdims=True)
        differ = chosen - fore * targets[:, k : k + 1]
        total += jnp.sum(jnp.where(jnp.abs(differ) < 1.0, 0.5 * differ * differ, jnp.abs(differ) - 0.5) * fore)
        slope = jnp.where(mask, fore * jnp.clip(differ, -1.0, 1.0), slope)
    return total, slope * (1.0 / count)


def per_device(
    feat_p2, feat_p3, feat_p4, feat_p5, rois, levels, labels, sampled, targets,
    fc1_w, fc1_m, fc1_v, fc2_w, fc2_m, fc2_v, head_w, head_m, head_v,
):
    side = feat_p2.shape[-1]
    channels = feat_p2.shape[1]
    boxes = rois.shape[2]
    images = lax.axis_size("wide")
    mine = boxes // lax.axis_size("narrow")
    first = lax.axis_index("narrow") * mine
    me = lax.axis_index("wide").astype(jnp.int32)
    feat = feature_rows((feat_p2, feat_p3, feat_p4, feat_p5))
    rank = box_order(rois[:, 0], levels[:, 0], side)
    table = box_table(rois[:, 0], levels[:, 0], rank, side)
    feats = lax.all_gather(feat, "wide", axis=0, tiled=True)
    tables = lax.all_gather(table, "wide", axis=0)
    w2 = lax.all_gather(fc2_w.astype(jnp.bfloat16), "narrow", axis=1, tiled=True)
    wh = lax.all_gather(head_w.astype(jnp.bfloat16), "narrow", axis=1, tiled=True)
    count = lax.psum(jnp.sum(sampled).astype(jnp.float32), "wide")

    def spans_of(t):
        return t[..., 6:8, 0].reshape(-1).astype(jnp.int32)

    zero = jnp.zeros((), jnp.int32)
    own = pool(feat, table[None], spans_of(table), zero, 1, channels)
    w1 = fc1_w.astype(jnp.bfloat16)
    part = lax.dot_general(own, w1, (((1,), (1,)), ((0,), (0,))), preferred_element_type=jnp.float32)
    pre1 = lax.psum_scatter(part, "narrow", scatter_dimension=1, tiled=True)
    other = pool(feats, tables, spans_of(tables), me + 1, images - 1, channels)

    hot = rank[:, None, :] == first + jnp.arange(mine, dtype=jnp.int32)[:, None]

    def pick(values):
        return jnp.sum(jnp.where(hot, values[:, 0][:, None, :], 0), axis=-1).reshape(-1)

    lab, samp = pick(labels), pick(sampled)
    tgt = jnp.stack([pick(targets[..., k]) for k in range(4)], axis=-1)

    def rows_by(left, right, dims):
        return lax.dot_general(left, right, (dims, ((0,), (0,))), preferred_element_type=jnp.float32)

    hid1 = jax.nn.silu(pre1).astype(jnp.bfloat16)
    pre2 = rows_by(hid1, w2, ((2,), (1,)))
    hid2 = jax.nn.silu(pre2).astype(jnp.bfloat16)
    logits = rows_by(hid2, wh, ((2,), (1,)))
    total, slope = loss_and_slope(logits.reshape(-1, logits.shape[-1]), lab, samp, tgt, count)
    back_z = slope.reshape(logits.shape).astype(jnp.bfloat16)
    back_h2 = rows_by(back_z, wh, ((2,), (2,)))
    back_p2 = (back_h2 * silu_slope(pre2)).astype(jnp.bfloat16)
    back_h1 = rows_by(back_p2, w2, ((2,), (2,)))
    back_p1 = (back_h1 * silu_slope(pre1)).astype(jnp.bfloat16)
    back = lax.all_gather(back_p1, ("wide", "narrow"), axis=1, tiled=True)
    grad_head = rows_by(hid2, back_z, ((1,), (1,)))
    grad_two = rows_by(hid1, back_p2, ((1,), (1,)))
    grad_two = lax.psum_scatter(grad_two, "narrow", scatter_dimension=1, tiled=True)
    grad_head = lax.psum_scatter(grad_head, "narrow", scatter_dimension=1, tiled=True)
    grad_two, grad_head = lax.psum((grad_two, grad_head), "wide")
    total = lax.psum(total, ("narrow", "wide"))
    new1 = update_first(me[None], own, other, back, fc1_w, fc1_m, fc1_v)
    new2 = adamw(fc2_w, fc2_m, fc2_v, grad_two)
    newh = adamw(head_w, head_m, head_v, grad_head)
    return (jnp.stack([total, count]),) + tuple(new1) + tuple(new2) + tuple(newh)


def solution(mesh):
    maps = P("wide", "narrow", None, None)
    rows = P(None, "narrow", None)
    box = P(None, "wide", None)
    coords = P(None, "wide", None, None)
    return jax.shard_map(
        per_device,
        mesh=mesh,
        in_specs=(maps,) * 4 + (coords, box, box, box, coords) + (rows,) * 9,
        out_specs=(P(),) + (rows,) * 9,
        check_vma=False,
    )
```

time: 2180 us -> 539 us (0.25)
  matrix products: 1120 us -> 30.2 us
  waiting for transfers between devices: 570 us -> 222 us
  local copies, waits for them, and re-layouts: 296 us -> 16 us
  Pallas kernels: 0 us -> 162 us
  other arithmetic: 80.3 us -> 14.6 us
  blocking collectives: 91.7 us -> 69 us
    dot_general x32 -> x8, matrix products: 1120 us -> 30.2 us  [the longest x6 19.5 us: rows_by(): lax.dot_general(left, right, (dims, ((0,), (0,))), preferred_element_type...]
    psum x1, waiting for transfers between devices: 434 us -> 0.01 us  [per_device(): grad_two, grad_head = lax.psum((grad_two, grad_head), 'wide')]
    transpose x8 -> x1, local copies, waits for them, and re-layouts: 253 us -> 0.03 us  [box_table(): jnp.stack(parts).transpose(2, 0, 1, 3).reshape(count // LANES, 2, 8, LANES)]
    pallas_call x0 -> x3, Pallas kernels: none -> 162 us  [the longest x2 116 us: pool(): pl.pallas_call(kernel, out_shape=jax.ShapeDtypeStruct((2, wide, steps * L...]
    reduce_scatter x4 -> x3, waiting for transfers between devices: 107 us -> 150 us  [the longest x1 75.6 us: per_device(): lax.psum_scatter(grad_two, 'narrow', scatter_dimension=1, tiled=True)]
    all_gather x1, waiting for transfers between devices: 0.01 us -> 39.4 us  [per_device(): lax.all_gather(fc2_w.astype(jnp.bfloat16), 'narrow', axis=1, tiled=True)]
    psum x2, blocking collectives: 91.7 us -> 54.8 us  [the longest x1 39.3 us: per_device(): total = lax.psum(total, ('narrow', 'wide'))]
    all_gather x1, waiting for transfers between devices: 0.02 us -> 32.6 us  [per_device(): lax.all_gather(head_w.astype(jnp.bfloat16), 'narrow', axis=1, tiled=True)]
  transfers between devices with their start and end apart: 9 -> 8, of which waited for: 5 -> 5; matrix products, arithmetic and copies ran while one was open for 66% -> 5% of each run, Pallas kernels for 0% -> 17%
where the time goes in v1:
time: 539 us; the launch traced here: 535 us
  waiting for transfers between devices  222 us (41%)
  Pallas kernels  162 us (30%)
  blocking collectives  69 us (13%)
  matrix products  30.2 us (6%)
  between operations  20.4 us (4%)
  local copies, waits for them, and re-layouts  16 us (3%)
  other arithmetic  14.6 us (3%)
    pallas_call x2, Pallas kernels, pool(): pl.pallas_call(kernel, out_shape=jax.ShapeDtypeStruct((2, wide, steps * L...  116 us
    reduce_scatter x1, waiting for transfers between devices, per_device(): lax.psum_scatter(grad_two, 'narrow', scatter_dimension=1, tiled=True)  75.6 us
    pallas_call x1, Pallas kernels, update_first(): pl.pallas_call(partial(update_kernel, images, boxes), out_shape=[jax.Shap...  45.9 us
    reduce_scatter x1, waiting for transfers between devices, per_device(): lax.psum_scatter(grad_head, 'narrow', scatter_dimension=1, tiled=True)  39.4 us
    all_gather x1, waiting for transfers between devices, per_device(): lax.all_gather(fc2_w.astype(jnp.bfloat16), 'narrow', axis=1, tiled=True)  39.4 us
    psum x1, blocking collectives, per_device(): total = lax.psum(total, ('narrow', 'wide'))  39.3 us
    reduce_scatter x1, waiting for transfers between devices, per_device(): pre1 = lax.psum_scatter(part, 'narrow', scatter_dimension=1, tiled=True)  34.6 us
    all_gather x1, waiting for transfers between devices, per_device(): lax.all_gather(head_w.astype(jnp.bfloat16), 'narrow', axis=1, tiled=True)  32.6 us
  transfers between devices with their start and end apart: 8, of which 5 were waited for; matrix products, arithmetic and copies ran while one was open for 5% of the time, Pallas kernels for 17%

profile of v1, /device:TPU:0, one launch (start us, length us, event | category | flops | bytes accessed | tf_op | source)
XLA Modules:
  0.0 535.2 jit_solution(11687102566864986220)
XLA Ops:
  8.1 0.9 bitcast_convert_fusion
  9.0 0.8 fusion.40
  9.8 0.7 bitcast_convert_fusion.1
  10.5 0.4 convert_reduce_fusion
  10.9 0.5 fusion.2
  11.4 0.1 squeeze.24
  11.5 0.1 select_n.276
  11.6 0.1 squeeze.25
  11.7 0.1 squeeze.26
  12.0 0.1 reduce_min.18
  12.1 0.1 reduce_max.27
  12.4 0.1 reshape.815
  12.5 0.1 broadcast_in_dim_reshape.4.refs_1_
  12.7 0.2 fusion.34
  12.9 0.1 gather.11.span_ref
  13.0 0.9 copy.177
  13.8 1.1 copy.176
  14.9 0.1 select_maximum_fusion
  15.1 0.4 copy.153
  15.5 0.3 reduce-precision_convert_fusion
  15.8 0.5 pad_maximum_fusion.refs_0_
  16.4 27.8 %pool_rois.2.own_ref = bf16[2,1568,512]{2,1,0:T(8,128)(2,1)S(1)} custom-call(s32[1]{0:T(128)} %constant.54.clone.1.order_ref, s32[16]{0:T(128)S(1)} %gather.11.span_ref, bf16[1,3840,128]{2,1,0:T(8,128)(2,1)S(1)} %pad_maximum_fusion.refs_0_, f32[1,4,2,8,128]{4,3,2,1,0:T(8,128)S(1)} %broadcast_in_dim_reshape.4.refs_1_), custom_call_target="tpu_custom_call" | custom-call | flops 3523215360 | bytes 3211264 | tf_op jit(solution)/shard_map/pool_rois/pallas_call | solution.py:93
  44.1 1.6 copy-done.2
  45.8 10.2 %fusion = f32[2,512,1024]{2,1,0:T(8,128)} fusion(bf16[2,1568,512]{2,1,0:T(8,128)(2,1)S(1)} %pool_rois.2.own_ref, f32[2,1568,1024]{2,1,0:T(8,128)} %w_ref.1), kind=kOutput, calls=%fused_computation.1 | convolution fusion | flops 3291545600 | bytes 20250624 | tf_op jit(solution)/shard_map/dot_general | solution.py:291
  56.1 1.1 copy-done.4
  57.2 0.9 convert_element_type.132
  58.2 0.8 convert_element_type.134
  59.1 0.6 reduce_sum.189
  60.4 15.6 %psum.29 = f32[]{:T(128)} all-reduce(f32[]{:T(128)S(6)} %convert_element_type.135), channel_id=1, replica_groups=mesh['narrow'=8,'wide'=4] {'wide'}, use_global_device_ids=true, to_apply=%region_26.27 | all-reduce | flops 1 | bytes 8 | tf_op jit(solution)/shard_map/psum | solution.py:283
  76.0 0.2 fusion.20
  77.0 0.2 fusion.25
  77.2 34.6 %reduce-scatter.4.cloned.1.call-done = f32[2,64,1024]{2,1,0:T(8,128)} async-done(((f32[2,512,1024]{2,1,0:T(8,128)}), f32[2,64,1024]{2,1,0:T(8,128)}) %reduce-scatter.4.cloned.1.call-update) | async-done | bytes 524304 | tf_op jit(solution)/shard_map/reduce_scatter | solution.py:292
  111.8 39.4 %all-gather.5.cloned.1.call-done = bf16[2,1024,1024]{2,1,0:T(8,128)(2,1)} async-done(((bf16[2,128,1024]{2,1,0:T(8,128)(2,1)}), bf16[2,1024,1024]{2,1,0:T(8,128)(2,1)}) %all-gather.5.cloned.1.call-update) | async-done | bytes 4194320 | tf_op jit(solution)/shard_map/all_gather | solution.py:281
  151.2 3.2 fusion.57
  154.4 32.6 %all-gather.7.cloned.1.call-done = bf16[2,1024,401]{1,0,2:T(2,128)(2,1)} async-done(((bf16[2,128,401]{1,0,2:T(2,128)(2,1)}), bf16[2,1024,401]{1,0,2:T(2,128)(2,1)}) %all-gather.7.cloned.1.call-update) | async-done | bytes 1642512 | tf_op jit(solution)/shard_map/all_gather | solution.py:282
  187.0 2.2 select_reduce_fusion.5
  189.2 0.5 select_reduce_fusion
  189.7 0.6 clamp_multiply_fusion.3
  190.3 0.6 fusion.48
  190.9 2.7 fusion.58
  193.6 0.2 reduce-scatter.6.cloned.1.call-start
  193.9 2.4 fusion.13
  196.3 4.7 fusion.56
  201.1 0.5 all-gather.9.cloned.1.call-update
  201.7 39.4 %reduce-scatter.8.cloned.1.call-done = f32[2,128,401]{1,2,0:T(8,128)} async-done(((f32[2,1024,401]{1,2,0:T(8,128)}), f32[2,128,401]{1,2,0:T(8,128)}) %reduce-scatter.8.cloned.1.call-update) | async-done | bytes 410640 | tf_op jit(solution)/shard_map/reduce_scatter | solution.py:320
  241.1 75.6 %reduce-scatter.6.cloned.1.call-done = f32[2,128,1024]{2,1,0:T(8,128)} async-done(((f32[2,1024,1024]{2,1,0:T(8,128)}), f32[2,128,1024]{2,1,0:T(8,128)}) %reduce-scatter.6.cloned.1.call-update) | async-done | bytes 1048592 | tf_op jit(solution)/shard_map/reduce_scatter | solution.py:319
  316.8 4.3 fusion.16
  321.1 14.1 %all_gather.17.refs_1_ = f32[4,4,2,8,128]{4,3,2,1,0:T(8,128)S(1)} all-gather(f32[1,4,2,8,128]{4,3,2,1,0:T(8,128)S(1)} %broadcast_in_dim_reshape.4.refs_1_), channel_id=1, replica_groups=mesh['narrow'=8,'wide'=4] {'wide'}, dimensions={0}, use_global_device_ids=true | all-gather | bytes 163840 | tf_op jit(solution)/shard_map/all_gather | solution.py:280
  335.3 0.2 copy.175
  335.5 0.1 copy.157
  335.6 0.1 copy.158
  335.7 0.6 gather_fusion
  336.3 0.1 select_n.298.span_ref
  336.5 2.1 copy-done.3
  338.6 88.7 %pool_rois.3.other_ref = bf16[2,1568,1536]{2,1,0:T(8,128)(2,1)S(1)} custom-call(s32[3]{0:T(128)S(1)} %compare_select_fusion.13.order_ref, s32[48]{0:T(128)S(1)} %select_n.298.span_ref, bf16[4,3840,128]{2,1,0:T(8,128)(2,1)S(1)} %copy-done.3, f32[4,4,2,8,128]{4,3,2,1,0:T(8,128)S(1)} %all_gather.17.refs_1_), custom_call_target="tpu_custom_call" | custom-call | flops 10569646080 | bytes 9633792 | tf_op jit(solution)/shard_map/pool_rois/pallas_call | solution.py:93
  427.2 3.7 copy-done
  434.2 39.3 %psum.28 = f32[1]{0:T(128)} all-reduce(f32[1]{0:T(128)} %bitcast.10), channel_id=1, replica_groups=mesh['narrow'=8,'wide'=4] {'narrow','wide'}, use_global_device_ids=true, to_apply=%region_24.25 | all-reduce | flops 1 | bytes 8 | tf_op jit(solution)/shard_map/psum | solution.py:322
  473.4 1.9 pad_maximum_fusion.1
  475.3 1.4 multiply_subtract_fusion.1
  476.8 1.0 copy.164
  477.7 1.0 copy.165
  478.7 1.0 copy.166
  479.7 2.3 multiply_subtract_fusion
  481.9 45.9 %update_first.1 = (f32[2,1568,1024]{2,1,0:T(8,128)}, f32[2,1568,1024]{2,1,0:T(8,128)}, f32[2,1568,1024]{2,1,0:T(8,128)}) custom-call(s32[1]{0:T(128)} %bitcast.12.me_ref, bf16[2,1568,512]{2,1,0:T(8,128)(2,1)} %copy-done.2, bf16[2,1568,1536]{2,1,0:T(8,128)(2,1)} %copy-done, bf16[2,2048,1024]{2,1,0:T(8,128)(2,1)} %all-gather.11.cloned.1.call-done.back_ref, ...), custom_call_target="tpu_custom_call" | custom-call | flops 13153337344 | bytes 98304000 | tf_op jit(solution)/shard_map/update_first/pallas_call | solution.py:209
  (81 shorter events, 1.2 us)
Async XLA Ops:
  8.0 6.9 %copy-start.10 = (f32[1,32,32,32]{3,2,1,0:T(8,128)S(1)}, f32[1,32,32,32]{3,2,1,0:T(8,128)}, u32[]{:S(2)}) copy-start(f32[1,32,32,32]{3,2,1,0:T(8,128)} %param.19) | copy-start | bytes 393220
  8.0 6.9 %copy-start.9 = (f32[1,32,64,64]{3,2,1,0:T(8,128)S(1)}, f32[1,32,64,64]{3,2,1,0:T(8,128)}, u32[]{:S(2)}) copy-start(f32[1,32,64,64]{3,2,1,0:T(8,128)} %param.18) | copy-start | bytes 1572868
  8.0 103.8 %reduce-scatter.4.cloned.1.call-start = ((), (), s32[]{:S(2)}) async-start(), calls=%async_computation.3 | async-start | bytes 4718592 | tf_op jit(solution)/shard_map/reduce_scatter | solution.py:292
  16.3 27.8 %copy-start.1 = (bf16[1,3840,128]{2,1,0:T(8,128)(2,1)}, bf16[1,3840,128]{2,1,0:T(8,128)(2,1)S(1)}, u32[]{:S(2)}) copy-start(bf16[1,3840,128]{2,1,0:T(8,128)(2,1)S(1)} %pad_maximum_fusion.refs_0_) | copy-start | bytes 2949124
  44.1 1.7 copy-start.2
  56.0 1.2 copy-start.4
  56.0 2.1 copy-start.5
  56.0 3.0 copy-start.14
  56.1 19.9 %copy-start.16 = (s32[2,1,512]{2,1,0:T(1,128)S(1)}, s32[2,1,512]{2,1,0:T(1,128)}, u32[]{:S(2)}) copy-start(s32[2,1,512]{2,1,0:T(1,128)} %param.24) | copy-start | bytes 12292
  56.1 20.8 %copy-start.15 = (f32[2,1,512,4]{2,3,1,0:T(4,128)S(1)}, f32[2,1,512,4]{2,3,1,0:T(4,128)}, u32[]{:S(2)}) copy-start(f32[2,1,512,4]{2,3,1,0:T(4,128)} %param.26) | copy-start | bytes 49156
  56.1 95.2 %all-gather.5.cloned.1.call-start = ((), (), s32[]{:S(2)}) async-start(), calls=%async_computation.4 | async-start | bytes 4718592 | tf_op jit(solution)/shard_map/all_gather | solution.py:281
  58.1 128.9 %all-gather.7.cloned.1.call-start = ((), (), s32[]{:S(2)}) async-start(), calls=%async_computation.5 | async-start | bytes 1847808 | tf_op jit(solution)/shard_map/all_gather | solution.py:282
  59.0 182.1 %reduce-scatter.8.cloned.1.call-start = ((), (), s32[]{:S(2)}) async-start(), calls=%async_computation.9 | async-start | bytes 3760128 | tf_op jit(solution)/shard_map/reduce_scatter | solution.py:320
  193.6 2.7 copy-start.11
  193.6 123.1 %reduce-scatter.6.cloned.1.call-start = ((), (), s32[]{:S(2)}) async-start(), calls=%async_computation.8 | async-start | bytes 9437184 | tf_op jit(solution)/shard_map/reduce_scatter | solution.py:319
  201.0 135.4 %all-gather.9.cloned.1.call-start = ((), (), s32[]{:S(2)}) async-start(), calls=%async_computation.6 | async-start | bytes 4915200 | tf_op jit(solution)/shard_map/all_gather | solution.py:279
  201.6 273.7 %all-reduce.6.cloned.1.call-start = ((), (), s32[]{:S(2)}) async-start(), calls=%async_computation.10 | async-start | bytes 2932736 | tf_op jit(solution)/shard_map/psum | solution.py:321
  316.7 165.2 %all-gather.11.cloned.1.call-start = ((), (), s32[]{:S(2)}) async-start(), calls=%async_computation.7 | async-start | bytes 8650752 | tf_op jit(solution)/shard_map/all_gather | solution.py:316
  336.4 2.1 copy-start.3
  338.6 136.8 %copy-start.12 = (f32[2,128,401]{1,0,2:T(2,128)S(1)}, f32[2,128,401]{1,0,2:T(2,128)}, u32[]{:S(2)}) copy-start(f32[2,128,401]{1,0,2:T(2,128)} %param.34) | copy-start | bytes 1231876
  338.6 136.8 %copy-start.13 = (f32[2,128,401]{1,0,2:T(2,128)S(1)}, f32[2,128,401]{1,0,2:T(2,128)}, u32[]{:S(2)}) copy-start(f32[2,128,401]{1,0,2:T(2,128)} %param.35) | copy-start | bytes 1231876
  427.2 3.7 copy-start
  475.3 4.3 copy-start.8
  476.8 2.9 copy-start.6
  476.8 2.9 copy-start.7
Sparse Core Ops, SparseCore 0:
  56.2 55.6 reduce-scatter.3
  114.5 36.7 all-gather.4
  153.8 33.1 all-gather.6
  193.7 47.2 reduce-scatter.7
  245.4 71.2 reduce-scatter.5
Sparse Core Ops, SparseCore 1:
  203.7 76.3 all-gather.8
  316.8 67.9 all-reduce.5
  388.5 77.9 all-gather.10

commit v2 on v1

--- a/solution.py
+++ b/solution.py
@@ -141,7 +141,7 @@
     return jnp.sum((key[..., :, None] > key[..., None, :]).astype(jnp.int32), axis=-1)
 
 
-def box_table(boxes, levels, rank, side):
+def box_table(boxes, levels, rank, side, sampled):
     count = boxes.shape[1]
     hot = (rank[:, None, :] == jnp.arange(count, dtype=jnp.int32)[:, None]).astype(jnp.bfloat16)
     both = jnp.concatenate([boxes, levels[..., None]], axis=-1).astype(jnp.bfloat16)
@@ -170,6 +170,8 @@
     chunks = jnp.floor((high - low + CHUNK) / CHUNK)
     first = jnp.maximum(jnp.minimum(low, rows - chunks * CHUNK), 0.0)
     parts = [split(v) for v in (y_start, y_step, top, base, x_start, x_step)]
+    lane = jnp.arange(half, dtype=jnp.int32)
+    first = jnp.where(lane == 1, jnp.sum(sampled).astype(jnp.float32), first)
     parts += [jnp.broadcast_to(v, parts[0].shape) for v in (first, chunks)]
     return jnp.stack(parts).transpose(2, 0, 1, 3).reshape(count // LANES, 2, 8, LANES)
 
@@ -234,32 +236,318 @@
     )(me, own, other, back, weight, moment, second)
 
 
-def silu_slope(value):
-    sig = jax.nn.sigmoid(value)
-    return sig * (1.0 + value * (1.0 - sig))
-
-
-def loss_and_slope(logits, labels, sampled, targets, count):
+def loss_and_slope(logits, box, count):
     place = lax.broadcasted_iota(jnp.int32, logits.shape, 1)
     is_class = place < CLASSES
-    weight = sampled.astype(jnp.float32)[:, None]
-    label = labels[:, None]
+    label = box[:, 0:1].astype(jnp.int32)
+    weight = box[:, 1:2]
     top = jnp.max(jnp.where(is_class, logits, -jnp.inf), axis=1, keepdims=True)
     grown = jnp.where(is_class, jnp.exp(jnp.where(is_class, logits - top, 0.0)), 0.0)
     norm = jnp.sum(grown, axis=1, keepdims=True)
     hot = place == label
     picked = jnp.sum(jnp.where(hot, logits, 0.0), axis=1, keepdims=True)
     fore = jnp.where(label > 0, weight, 0.0)
-    total = jnp.sum(weight * (top + jnp.log(norm) - picked))
-    slope = weight * (grown / norm - hot.astype(jnp.float32))
+    rows = weight * (top + jnp.log(norm) - picked)
+    slope = weight * (grown / norm - jnp.where(hot, 1.0, 0.0))
+    offset = place - (CLASSES + 4 * (label - 1))
     for k in range(4):
-        mask = place == CLASSES + 4 * (label - 1) + k
-        mask = mask & (label > 0)
-        chosen = fore * jnp.sum(jnp.where(mask, logits, 0.0), axis=1, keepdims=True)
-        differ = chosen - fore * targets[:, k : k + 1]
-        total += jnp.sum(jnp.where(jnp.abs(differ) < 1.0, 0.5 * differ * differ, jnp.abs(differ) - 0.5) * fore)
+        mask = (offset == k) & (place >= CLASSES)
+        chosen = jnp.sum(jnp.where(mask, logits, 0.0), axis=1, keepdims=True)
+        differ = fore * (chosen - box[:, 2 + k : 3 + k])
+        near = jnp.abs(differ)
+        rows += jnp.where(near < 1.0, 0.5 * differ * differ, near - 0.5) * fore
         slope = jnp.where(mask, fore * jnp.clip(differ, -1.0, 1.0), slope)
-    return total, slope * (1.0 / count)
+    return rows, slope / count
+
+
+def sigmoid(value):
+    return 1.0 / (1.0 + jnp.exp(-value))
+
+
+def head_kernel(
+    images, parts, mine,
+    part_ref, w2_ref, wh_ref, box_ref, count_ref,
+    back_ref, hid1_ref, hid2_ref, slope2_ref, slopez_ref, loss_ref,
+    sums, landed, own, rs_send, rs_recv, ag_send, ag_recv, up_send, up_recv, down_send, down_recv, own_sem,
+):
+    me = lax.axis_index("narrow")
+    level = lax.axis_index("wide")
+    bits = parts.bit_length() - 1
+    turn = [(1 - 2 * ((me // 2**k) % 2)) * 2**k for k in range(bits)]
+
+    def peer(mask):
+        return me + sum((turn[k] for k in range(bits) if mask >> k & 1), 0)
+
+    links = list(range(1, bits))
+    orders = [links, links[::-1]]
+
+    barrier = pltpu.get_barrier_semaphore()
+    for k in range(bits):
+        pl.semaphore_signal(barrier, inc=1, device_id={"narrow": peer(1 << k)})
+
+    @pl.when(level > 0)
+    def _():
+        pl.semaphore_signal(barrier, inc=1, device_id={"wide": level - 1})
+
+    @pl.when(level < images - 1)
+    def _():
+        pl.semaphore_signal(barrier, inc=1, device_id={"wide": level + 1})
+
+    ends = jnp.where(level > 0, 1, 0) + jnp.where(level < images - 1, 1, 0)
+    pl.semaphore_wait(barrier, bits + ends)
+
+    def scatter(p, mask, bit, source):
+        return pltpu.make_async_remote_copy(
+            src_ref=source,
+            dst_ref=landed.at[p, mask],
+            send_sem=rs_send.at[p, mask],
+            recv_sem=rs_recv.at[p, mask],
+            device_id={"narrow": peer(1 << bit)},
+        )
+
+    def part_at(p, mask):
+        return part_ref.at[p, pl.ds(pl.multiple_of(peer(mask) * mine, mine), mine), :]
+
+    copies = {}
+    for p in range(2):
+        for mask in range(1, parts, 2):
+            copies[p, mask] = scatter(p, mask, 0, part_at(p, mask))
+            copies[p, mask].start()
+
+    def stage(p, at):
+        order = [0] + orders[p]
+        bit = order[at - 1]
+        seen = sum(1 << b for b in order[:at])
+        for mask in range(parts):
+            if mask & seen:
+                continue
+            copies[p, mask | 1 << bit].wait_recv()
+            if at == 1:
+                have = part_ref[p, pl.ds(pl.multiple_of(peer(mask) * mine, mine), mine), :]
+            else:
+                have = sums[p, mask]
+            sums[p, mask] = have + landed[p, mask | 1 << bit]
+            if at < bits and mask >> order[at] & 1:
+                copies[p, mask] = scatter(p, mask, order[at], sums.at[p, mask])
+                copies[p, mask].start()
+
+    for at in range(1, bits):
+        for p in range(2):
+            stage(p, at)
+
+    def rows(p, image, mask):
+        place = (image * parts + peer(mask)) * mine
+        return back_ref.at[p, pl.ds(pl.multiple_of(place, mine), mine), :]
+
+    def spread(p, image, mask, bit, source=None):
+        spot = rows(p, image, mask)
+        there = mask | 1 << bit
+        return pltpu.make_async_remote_copy(
+            src_ref=spot if source is None else source,
+            dst_ref=spot,
+            send_sem=ag_send.at[p, image, there],
+            recv_sem=ag_recv.at[p, image, there],
+            device_id={"narrow": peer(1 << bit)},
+        )
+
+    def arrive(p, image, mask):
+        spot = rows(p, image, mask)
+        pltpu.make_async_remote_copy(
+            src_ref=spot, dst_ref=spot, send_sem=ag_send.at[p, image, mask],
+            recv_sem=ag_recv.at[p, image, mask], device_id={"narrow": peer(1)},
+        ).wait_recv()
+
+    def hop(p, d, up, source=None):
+        image = level - d if up else level + d
+        spot = rows(p, image, 0)
+        return pltpu.make_async_remote_copy(
+            src_ref=spot if source is None else source,
+            dst_ref=spot,
+            send_sem=(up_send if up else down_send).at[p, d],
+            recv_sem=(up_recv if up else down_recv).at[p, d],
+            device_id={"wide": level + 1 if up else level - 1},
+        )
+
+    def came(p, d, up):
+        image = level - d if up else level + d
+        spot = rows(p, image, 0)
+        pltpu.make_async_remote_copy(
+            src_ref=spot, dst_ref=spot, send_sem=(up_send if up else down_send).at[p, d],
+            recv_sem=(up_recv if up else down_recv).at[p, d - 1],
+            device_id={"wide": level - 1 if up else level + 1},
+        ).wait_recv()
+
+    steps = [orders[p] + [0] for p in range(2)]
+
+    def masks_before(p, at):
+        seen = sum(1 << b for b in steps[p][:at])
+        return [m for m in range(parts) if not m & ~seen]
+
+    def advance(p, image, at, source=None):
+        bit = steps[p][at]
+        if at:
+            last = steps[p][at - 1]
+            for m in masks_before(p, at - 1):
+                arrive(p, image, m | 1 << last)
+        for m in masks_before(p, at):
+            spread(p, image, m, bit, source if m == 0 else None).start()
+
+    def finish(p, image):
+        last = steps[p][-1]
+        for m in masks_before(p, bits - 1):
+            arrive(p, image, m | 1 << last)
+        for at in range(bits):
+            for m in masks_before(p, at):
+                spread(p, image, m, steps[p][at]).wait_send()
+
+    count = count_ref[0:1, 0:1]
+    for p in range(2):
+        stage(p, bits)
+        pre1 = sums[p, 0]
+        sig1 = sigmoid(pre1)
+        hid1 = (pre1 * sig1).astype(jnp.bfloat16)
+        pre2 = jnp.dot(hid1, w2_ref[p], preferred_element_type=jnp.float32)
+        sig2 = sigmoid(pre2)
+        hid2 = (pre2 * sig2).astype(jnp.bfloat16)
+        logits = jnp.dot(hid2, wh_ref[p], preferred_element_type=jnp.float32)
+        loss, slope = loss_and_slope(logits, box_ref[p], count)
+        loss_ref[p] = jnp.broadcast_to(loss, loss_ref.shape[1:])
+        back_z = slope.astype(jnp.bfloat16)
+        turned = (((1,), (1,)), ((), ()))
+        back_h2 = lax.dot_general(back_z, wh_ref[p], turned, preferred_element_type=jnp.float32)
+        back_p2 = (back_h2 * (sig2 * (1.0 + pre2 * (1.0 - sig2)))).astype(jnp.bfloat16)
+        back_h1 = lax.dot_general(back_p2, w2_ref[p], turned, preferred_element_type=jnp.float32)
+        own[p] = (back_h1 * (sig1 * (1.0 + pre1 * (1.0 - sig1)))).astype(jnp.bfloat16)
+
+        @pl.when(level < images - 1)
+        def _():
+            hop(p, 0, True, own.at[p]).start()
+
+        @pl.when(level > 0)
+        def _():
+            hop(p, 0, False, own.at[p]).start()
+
+        advance(p, level, 0, own.at[p])
+        pltpu.make_async_copy(own.at[p], rows(p, level, 0), own_sem.at[p]).start()
+        hid1_ref[p] = hid1
+        hid2_ref[p] = hid2
+        slope2_ref[p] = back_p2
+        slopez_ref[p] = back_z
+    for p in range(2):
+        pltpu.make_async_copy(own.at[p], rows(p, level, 0), own_sem.at[p]).wait()
+
+    def each_side(d, do):
+        @pl.when(level >= d)
+        def _():
+            do(level - d, True)
+
+        @pl.when(level + d < images)
+        def _():
+            do(level + d, False)
+
+    def enter(d):
+        def do(image, up):
+            for p in range(2):
+                came(p, d, up)
+
+                @pl.when((level < images - 1) if up else (level > 0))
+                def _():
+                    hop(p, d, up).start()
+
+                advance(p, image, 0)
+
+        each_side(d, do)
+
+    def go_on(d, at):
+        if d == 0:
+            for p in range(2):
+                advance(p, level, at)
+        else:
+
+            def do(image, up):
+                for p in range(2):
+                    advance(p, image, at)
+
+            each_side(d, do)
+
+    for tick in range(1, images + bits - 1):
+        for d in range(images):
+            at = tick - d
+            if at == 0:
+                enter(d)
+            elif 0 < at < bits:
+                go_on(d, at)
+
+    for p in range(2):
+        finish(p, level)
+
+        @pl.when(level < images - 1)
+        def _():
+            hop(p, 0, True).wait_send()
+
+        @pl.when(level > 0)
+        def _():
+            hop(p, 0, False).wait_send()
+
+    for d in range(1, images):
+
+        def do(image, up):
+            for p in range(2):
+                finish(p, image)
+
+                @pl.when((level < images - 1) if up else (level > 0))
+                def _():
+                    hop(p, d, up).wait_send()
+
+        each_side(d, do)
+    for p in range(2):
+        for mask in range(1, parts):
+            copies[p, mask].wait_send()
+
+
+def head_step(part, w2, wh, box, count, images, parts):
+    passes, boxes, hidden = part.shape
+    mine = boxes // parts
+    outs = wh.shape[2]
+    low = jnp.bfloat16
+    vmem = pl.BlockSpec(memory_space=pltpu.VMEM)
+    dma = pltpu.SemaphoreType.DMA
+    return pl.pallas_call(
+        partial(head_kernel, images, parts, mine),
+        out_shape=[
+            jax.ShapeDtypeStruct((passes, images * boxes, hidden), low),
+            jax.ShapeDtypeStruct((passes, mine, hidden), low),
+            jax.ShapeDtypeStruct((passes, mine, hidden), low),
+            jax.ShapeDtypeStruct((passes, mine, hidden), low),
+            jax.ShapeDtypeStruct((passes, mine, outs), low),
+            jax.ShapeDtypeStruct((passes, mine, LANES), jnp.float32),
+        ],
+        in_specs=[vmem] * 5,
+        out_specs=[pl.BlockSpec(memory_space=pl.ANY)] + [vmem] * 5,
+        scratch_shapes=[
+            pltpu.VMEM((passes, parts, mine, hidden), jnp.float32),
+            pltpu.VMEM((passes, parts, mine, hidden), jnp.float32),
+            pltpu.VMEM((passes, mine, hidden), low),
+            dma((passes, parts)),
+            dma((passes, parts)),
+            dma((passes, images, parts)),
+            dma((passes, images, parts)),
+            dma((passes, images)),
+            dma((passes, images)),
+            dma((passes, images)),
+            dma((passes, images)),
+            dma((passes,)),
+        ],
+        compiler_params=pltpu.CompilerParams(
+            vmem_limit_bytes=48 * MIB, collective_id=0, has_side_effects=True
+        ),
+        cost_estimate=pl.CostEstimate(
+            flops=8 * passes * mine * hidden * (hidden + outs),
+            bytes_accessed=100 * MIB,
+            transcendentals=4 * passes * mine * hidden,
+        ),
+        name="head_step",
+    )(part, w2, wh, box, count)
 
 
 def per_device(
@@ -275,12 +563,14 @@
     me = lax.axis_index("wide").astype(jnp.int32)
     feat = feature_rows((feat_p2, feat_p3, feat_p4, feat_p5))
     rank = box_order(rois[:, 0], levels[:, 0], side)
-    table = box_table(rois[:, 0], levels[:, 0], rank, side)
+    table = box_table(rois[:, 0], levels[:, 0], rank, side, sampled)
     feats = lax.all_gather(feat, "wide", axis=0, tiled=True)
     tables = lax.all_gather(table, "wide", axis=0)
+    outs = head_w.shape[2]
     w2 = lax.all_gather(fc2_w.astype(jnp.bfloat16), "narrow", axis=1, tiled=True)
-    wh = lax.all_gather(head_w.astype(jnp.bfloat16), "narrow", axis=1, tiled=True)
-    count = lax.psum(jnp.sum(sampled).astype(jnp.float32), "wide")
+    wide_head = jnp.pad(head_w, ((0, 0), (0, 0), (0, -outs % LANES))).astype(jnp.bfloat16)
+    wh = lax.all_gather(wide_head, "narrow", axis=1, tiled=True)
+    count = jnp.sum(tables[:, 0, 0, 6, 1])
 
     def spans_of(t):
         return t[..., 6:8, 0].reshape(-1).astype(jnp.int32)
@@ -289,37 +579,29 @@
     own = pool(feat, table[None], spans_of(table), zero, 1, channels)
     w1 = fc1_w.astype(jnp.bfloat16)
     part = lax.dot_general(own, w1, (((1,), (1,)), ((0,), (0,))), preferred_element_type=jnp.float32)
-    pre1 = lax.psum_scatter(part, "narrow", scatter_dimension=1, tiled=True)
+    hot = rank[:, None, :] == first + jnp.arange(mine, dtype=jnp.int32)[:, None]
+
+    def pick(values):
+        return jnp.sum(jnp.where(hot, values[:, 0].astype(jnp.float32)[:, None, :], 0), axis=-1)
+
+    box = [pick(labels), pick(sampled)] + [pick(targets[..., k]) for k in range(4)]
+    box = jnp.pad(jnp.stack(box, axis=-1), ((0, 0), (0, 0), (0, LANES - 6)))
+    back, hid1, hid2, back_p2, back_z, loss = head_step(
+        part, w2, wh, box, jnp.full((8, LANES), count), images, boxes // mine
+    )
     other = pool(feats, tables, spans_of(tables), me + 1, images - 1, channels)
 
-    hot = rank[:, None, :] == first + jnp.arange(mine, dtype=jnp.int32)[:, None]
-
-    def pick(values):
-        return jnp.sum(jnp.where(hot, values[:, 0][:, None, :], 0), axis=-1).reshape(-1)
-
-    lab, samp = pick(labels), pick(sampled)
-    tgt = jnp.stack([pick(targets[..., k]) for k in range(4)], axis=-1)
-
-    def rows_by(left, right, dims):
-        return lax.dot_general(left, right, (dims, ((0,), (0,))), preferred_element_type=jnp.float32)
-
-    hid1 = jax.nn.silu(pre1).astype(jnp.bfloat16)
-    pre2 = rows_by(hid1, w2, ((2,), (1,)))
-    hid2 = jax.nn.silu(pre2).astype(jnp.bfloat16)
-    logits = rows_by(hid2, wh, ((2,), (1,)))
-    total, slope = loss_and_slope(logits.reshape(-1, logits.shape[-1]), lab, samp, tgt, count)
-    back_z = slope.reshape(logits.shape).astype(jnp.bfloat16)
-    back_h2 = rows_by(back_z, wh, ((2,), (2,)))
-    back_p2 = (back_h2 * silu_slope(pre2)).astype(jnp.bfloat16)
-    back_h1 = rows_by(back_p2, w2, ((2,), (2,)))
-    back_p1 = (back_h1 * silu_slope(pre1)).astype(jnp.bfloat16)
-    back = lax.all_gather(back_p1, ("wide", "narrow"), axis=1, tiled=True)
-    grad_head = rows_by(hid2, back_z, ((1,), (1,)))
-    grad_two = rows_by(hid1, back_p2, ((1,), (1,)))
-    grad_two = lax.psum_scatter(grad_two, "narrow", scatter_dimension=1, tiled=True)
-    grad_head = lax.psum_scatter(grad_head, "narrow", scatter_dimension=1, tiled=True)
-    grad_two, grad_head = lax.psum((grad_two, grad_head), "wide")
-    total = lax.psum(total, ("narrow", "wide"))
+    def rows_by(left, right):
+        return lax.dot_general(left, right, (((1,), (1,)), ((0,), (0,))), preferred_element_type=jnp.float32)
+
+    def over_all(grad):
+        grad = lax.psum_scatter(grad, "narrow", scatter_dimension=1, tiled=True)
+        grad = lax.psum_scatter(grad, "wide", scatter_dimension=1, tiled=True)
+        return lax.all_gather(grad, "wide", axis=1, tiled=True)
+
+    grad_two = over_all(rows_by(hid1, back_p2))
+    grad_head = over_all(rows_by(hid2, back_z))[..., :outs]
+    total = jnp.sum(lax.all_gather(jnp.sum(loss[:, :, 0]).reshape(1, 1), ("wide", "narrow"), axis=0, tiled=True))
     new1 = update_first(me[None], own, other, back, fc1_w, fc1_m, fc1_v)
     new2 = adamw(fc2_w, fc2_m, fc2_v, grad_two)
     newh = adamw(head_w, head_m, head_v, grad_head)

time: 539 us -> 504 us (0.935)
  waiting for transfers between devices: 222 us -> 126 us
  Pallas kernels: 162 us -> 238 us
  matrix products: 30.2 us -> 18.8 us
    pallas_call x0 -> x1, Pallas kernels: none -> 73.5 us  [head_step(): pl.pallas_call(partial(head_kernel, images, parts, mine), out_shape=[jax....]
    psum x2 -> x0, blocking collectives: 54.8 us -> none  [the longest x1 39.3 us: per_device(): total = lax.psum(total, ('narrow', 'wide'))]
    unnamed x0 -> x1, blocking collectives: none -> 39.4 us
    all_gather x1, waiting for transfers between devices: 39.4 us -> 5.66 us  [per_device(): lax.all_gather(fc2_w.astype(jnp.bfloat16), 'narrow', axis=1, tiled=True)]
    all_gather x2, waiting for transfers between devices: 32.6 us -> 0.01 us  [the longest x1 0.01 us: per_device(): wh = lax.all_gather(wide_head, 'narrow', axis=1, tiled=True)]
    reduce_scatter x3 -> x4, waiting for transfers between devices: 150 us -> 119 us  [the longest x2 119 us: over_all(): grad = lax.psum_scatter(grad, 'narrow', scatter_dimension=1, tiled=True)]
    all_gather x0 -> x1, blocking collectives: none -> 16 us  [over_all(): return lax.all_gather(grad, 'wide', axis=1, tiled=True)]
    dot_general x6 -> x2, matrix products: 19.5 us -> 7.46 us  [rows_by(): lax.dot_general(left, right, (((1,), (1,)), ((0,), (0,))), preferred_elem...]
  transfers between devices with their start and end apart: 8 -> 8, of which waited for: 5 -> 3; matrix products, arithmetic and copies ran while one was open for 5% -> 6% of each run, Pallas kernels for 17% -> 33%
where the time goes in v2:
time: 504 us; the launch traced here: 503 us
  Pallas kernels  238 us (47%)
  waiting for transfers between devices  126 us (25%)
  blocking collectives  70.5 us (14%)
  local copies, waits for them, and re-layouts  19.3 us (4%)
  matrix products  18.8 us (4%)
  between operations  16.8 us (3%)
  other arithmetic  13.6 us (3%)
    reduce_scatter x2, waiting for transfers between devices, over_all(): grad = lax.psum_scatter(grad, 'narrow', scatter_dimension=1, tiled=True)  119 us
    pallas_call x2, Pallas kernels, pool(): pl.pallas_call(kernel, out_shape=jax.ShapeDtypeStruct((2, wide, steps * L...  119 us
    pallas_call x1, Pallas kernels, head_step(): pl.pallas_call(partial(head_kernel, images, parts, mine), out_shape=[jax....  73.5 us
    pallas_call x1, Pallas kernels, update_first(): pl.pallas_call(partial(update_kernel, images, boxes), out_shape=[jax.Shap...  46 us
    unnamed x1, blocking collectives  39.4 us
    all_gather x1, blocking collectives, over_all(): return lax.all_gather(grad, 'wide', axis=1, tiled=True)  16 us
    unnamed x63, local copies, waits for them, and re-layouts  15.5 us
    all_gather x1, blocking collectives, per_device(): tables = lax.all_gather(table, 'wide', axis=0)  15.1 us
  transfers between devices with their start and end apart: 8, of which 3 were waited for; matrix products, arithmetic and copies ran while one was open for 6% of the time, Pallas kernels for 33%

profile of v2, /device:TPU:0, one launch (start us, length us, event | category | flops | bytes accessed | tf_op | source)
XLA Modules:
  0.0 503.2 jit_solution(704716999269836182)
XLA Ops:
  8.1 1.2 convert.12
  9.3 0.2 copy.169
  9.5 0.7 pad.24
  10.3 0.9 convert_element_type.91
  11.4 0.4 convert_reduce_fusion
  11.8 0.5 fusion.2
  12.3 0.1 squeeze.11
  12.4 0.1 select_n.172
  12.5 0.1 squeeze.12
  12.7 0.6 fusion.36
  14.0 0.1 reduce_min.18
  14.2 0.1 reduce_max.18
  14.4 0.1 squeeze.13
  14.7 0.1 broadcast_in_dim_reshape.3.refs_1_
  14.8 0.1 reshape.469
  14.9 0.2 fusion.18
  15.1 0.1 gather.11.span_ref
  15.2 0.1 copy.191
  15.3 0.2 copy.190
  15.5 0.1 select_maximum_fusion
  15.7 0.4 copy.167
  16.1 0.3 copy-done.18
  16.5 0.3 fusion.14
  16.8 0.1 copy.170
  17.0 15.1 %all_gather.23.refs_1_ = f32[4,4,2,8,128]{4,3,2,1,0:T(8,128)S(1)} all-gather(f32[1,4,2,8,128]{4,3,2,1,0:T(8,128)S(1)} %broadcast_in_dim_reshape.3.refs_1_), channel_id=1, replica_groups=mesh['narrow'=8,'wide'=4] {'wide'}, dimensions={0}, use_global_device_ids=true | all-gather | bytes 163840 | tf_op jit(solution)/shard_map/all_gather | solution.py:568
  32.0 0.7 slice_reduce_fusion.1
  32.7 0.3 reduce-precision_convert_fusion
  33.0 0.5 pad_maximum_fusion.refs_0_
  33.6 29.4 %pool_rois.2.own_ref = bf16[2,1568,512]{2,1,0:T(8,128)(2,1)S(1)} custom-call(s32[1]{0:T(128)} %constant.40.clone.1.order_ref, s32[16]{0:T(128)S(1)} %gather.11.span_ref, bf16[1,3840,128]{2,1,0:T(8,128)(2,1)S(1)} %pad_maximum_fusion.refs_0_, f32[1,4,2,8,128]{4,3,2,1,0:T(8,128)S(1)} %broadcast_in_dim_reshape.3.refs_1_), custom_call_target="tpu_custom_call" | custom-call | flops 3523215360 | bytes 3211264 | tf_op jit(solution)/shard_map/pool_rois/pallas_call | solution.py:93
  63.0 1.6 copy-done.2
  64.6 10.9 %fusion.part_ref = f32[2,512,1024]{2,1,0:T(8,128)} fusion(bf16[2,1568,512]{2,1,0:T(8,128)(2,1)S(1)} %pool_rois.2.own_ref, f32[2,1568,1024]{2,1,0:T(8,128)} %w_ref.1), kind=kOutput, calls=%fused_computation.1 | convolution fusion | flops 3291545600 | bytes 20250624 | tf_op jit(solution)/shard_map/dot_general | solution.py:581
  75.6 5.7 %all-gather.5.cloned.1.call-done.w2_ref = bf16[2,1024,1024]{2,1,0:T(8,128)(2,1)} async-done(((bf16[2,128,1024]{2,1,0:T(8,128)(2,1)}), bf16[2,1024,1024]{2,1,0:T(8,128)(2,1)}) %all-gather.5.cloned.1.call-update) | async-done | bytes 4194320 | tf_op jit(solution)/shard_map/all_gather | solution.py:570
  81.2 0.6 broadcast_in_dim.136.count_ref
  81.9 1.6 copy-done.3
  83.5 73.5 %head_step.1 = (bf16[2,2048,1024]{2,1,0:T(8,128)(2,1)}, bf16[2,64,1024]{2,1,0:T(8,128)(2,1)S(1)}, bf16[2,64,1024]{2,1,0:T(8,128)(2,1)S(1)}, bf16[2,64,1024]{2,1,...) custom-call(f32[2,512,1024]{2,1,0:T(8,128)} %fusion.part_ref, ...), custom_call_target="tpu_custom_call" | custom-call | flops 1610612736 | bytes 104857600 | tf_op jit(solution)/shard_map/head_step/pallas_call | solution.py:515
  156.9 4.7 fusion.37
  161.7 2.8 fusion.38
  164.6 0.5 all-gather.9.cloned.1.call-update
  165.2 68.3 %reduce-scatter.5.cloned.1.call-done = f32[2,128,1024]{2,1,0:T(8,128)} async-done(((f32[2,1024,1024]{2,1,0:T(8,128)}), f32[2,128,1024]{2,1,0:T(8,128)}) %reduce-scatter.5.cloned.1.call-update) | async-done | bytes 1048592 | tf_op jit(solution)/shard_map/reduce_scatter | solution.py:598
  233.5 0.2 copy.177
  233.8 0.2 copy.189
  234.0 0.1 copy.172
  234.1 0.1 copy.173
  234.2 0.6 gather_fusion
  234.8 0.1 select_n.183.span_ref
  234.9 0.2 copy.174
  235.2 0.2 copy.175
  235.4 0.6 dynamic-slice
  236.0 0.6 slice_reduce_fusion
  236.6 1.4 dynamic-update-slice
  238.0 50.9 %reduce-scatter.9.cloned.1.call-done = f32[2,128,512]{2,1,0:T(8,128)} async-done(((f32[2,1024,512]{2,1,0:T(8,128)}), f32[2,128,512]{2,1,0:T(8,128)}) %reduce-scatter.9.cloned.1.call-update) | async-done | bytes 524304 | tf_op jit(solution)/shard_map/reduce_scatter | solution.py:598
  289.0 2.1 copy-done.4
  291.2 89.5 %pool_rois.3.other_ref = bf16[2,1568,1536]{2,1,0:T(8,128)(2,1)S(1)} custom-call(s32[3]{0:T(128)S(1)} %compare_select_fusion.13.order_ref, s32[48]{0:T(128)S(1)} %select_n.183.span_ref, bf16[4,3840,128]{2,1,0:T(8,128)(2,1)S(1)} %copy-done.4, f32[4,4,2,8,128]{4,3,2,1,0:T(8,128)S(1)} %all_gather.23.refs_1_), custom_call_target="tpu_custom_call" | custom-call | flops 10569646080 | bytes 9633792 | tf_op jit(solution)/shard_map/pool_rois/pallas_call | solution.py:93
  380.7 3.7 copy-done
  384.3 39.4 %all-reduce.5 = f32[32]{0:T(128)S(1)} all-reduce(f32[32]{0:T(128)S(1)} %dynamic-update-slice), channel_id=1, replica_groups=mesh['narrow'=8,'wide'=4] {'wide','narrow'}, use_global_device_ids=true, to_apply=%add.5 | all-reduce | flops 32 | bytes 256
  423.8 0.6 reduce.6
  424.4 1.9 pad_maximum_fusion.1
  426.3 46.0 %update_first.1 = (f32[2,1568,1024]{2,1,0:T(8,128)}, f32[2,1568,1024]{2,1,0:T(8,128)}, f32[2,1568,1024]{2,1,0:T(8,128)}) custom-call(s32[1]{0:T(128)} %bitcast.20.me_ref, bf16[2,1568,512]{2,1,0:T(8,128)(2,1)} %copy-done.2, bf16[2,1568,1536]{2,1,0:T(8,128)(2,1)} %copy-done, bf16[2,2048,1024]{2,1,0:T(8,128)(2,1)} %get-tuple-element.20.back_ref, ...), custom_call_target="tpu_custom_call" | custom-call | flops 13153337344 | bytes 98304000 | tf_op jit(solution)/shard_map/update_first/pallas_call | solution.py:211
  472.3 16.0 %all_gather.27 = f32[2,128,512]{2,1,0:T(8,128)S(1)} all-gather(f32[2,32,512]{2,1,0:T(8,128)} %reduce-scatter.11.cloned.1.call-done), channel_id=1, replica_groups=mesh['narrow'=8,'wide'=4] {'wide'}, dimensions={1}, use_global_device_ids=true | all-gather | bytes 655360 | tf_op jit(solution)/shard_map/all_gather | solution.py:600
  488.3 0.4 multiply_subtract_fusion.1
  488.7 1.0 copy.178
  489.7 1.0 copy.179
  490.7 1.0 copy.180
  491.6 4.2 multiply_subtract_fusion
  (98 shorter events, 1.4 us)
Async XLA Ops:
  8.0 2.3 copy-start.5
  8.0 3.3 copy-start.16
  8.0 3.3 copy-start.13
  8.0 67.5 %all-gather.7.cloned.1.call-start = ((), (), s32[]{:S(2)}) async-start(), calls=%async_computation.5 | async-start | bytes 2359296 | tf_op jit(solution)/shard_map/all_gather | solution.py:572
  9.3 3.4 copy-start.17
  9.5 5.7 %copy-start.14 = (f32[1,32,8,8]{1,3,2,0:T(8,128)S(1)}, f32[1,32,8,8]{1,3,2,0:T(8,128)}, u32[]{:S(2)}) copy-start(f32[1,32,8,8]{1,3,2,0:T(8,128)} %param.21) | copy-start | bytes 24580
  9.5 5.8 %copy-start.12 = (f32[1,32,16,16]{1,3,2,0:T(8,128)S(1)}, f32[1,32,16,16]{1,3,2,0:T(8,128)}, u32[]{:S(2)}) copy-start(f32[1,32,16,16]{1,3,2,0:T(8,128)} %param.20) | copy-start | bytes 98308
  10.3 5.2 %copy-start.8 = (f32[1,32,64,64]{3,2,1,0:T(8,128)S(1)}, f32[1,32,64,64]{3,2,1,0:T(8,128)}, u32[]{:S(2)}) copy-start(f32[1,32,64,64]{3,2,1,0:T(8,128)} %param.18) | copy-start | bytes 1572868
  10.3 5.3 %copy-start.9 = (f32[1,32,32,32]{3,2,1,0:T(8,128)S(1)}, f32[1,32,32,32]{3,2,1,0:T(8,128)}, u32[]{:S(2)}) copy-start(f32[1,32,32,32]{3,2,1,0:T(8,128)} %param.19) | copy-start | bytes 393220
  10.3 70.9 %all-gather.5.cloned.1.call-start = ((), (), s32[]{:S(2)}) async-start(), calls=%async_computation.4 | async-start | bytes 4718592 | tf_op jit(solution)/shard_map/all_gather | solution.py:570
  11.2 222.2 %reduce-scatter.5.cloned.1.call-start = ((), (), s32[]{:S(2)}) async-start(), calls=%async_computation.7 | async-start | bytes 9437184 | tf_op jit(solution)/shard_map/reduce_scatter | solution.py:598
  15.7 0.7 copy-start.18
  15.7 0.7 copy-start.15
  33.6 29.4 %copy-start.1 = (bf16[1,3840,128]{2,1,0:T(8,128)(2,1)}, bf16[1,3840,128]{2,1,0:T(8,128)(2,1)S(1)}, u32[]{:S(2)}) copy-start(bf16[1,3840,128]{2,1,0:T(8,128)(2,1)S(1)} %pad_maximum_fusion.refs_0_) | copy-start | bytes 2949124
  63.0 1.7 copy-start.2
  81.9 1.6 copy-start.3
  161.6 127.3 %reduce-scatter.9.cloned.1.call-start = ((), (), s32[]{:S(2)}) async-start(), calls=%async_computation.10 | async-start | bytes 4718592 | tf_op jit(solution)/shard_map/reduce_scatter | solution.py:598
  164.5 69.1 %copy-start.7 = (f32[2,128,401]{1,0,2:T(2,128)S(1)}, f32[2,128,401]{1,0,2:T(2,128)}, u32[]{:S(2)}) copy-start(f32[2,128,401]{1,0,2:T(2,128)} %param.33) | copy-start | bytes 1231876
  164.5 70.4 %copy-start.10 = (f32[2,128,401]{1,0,2:T(2,128)S(1)}, f32[2,128,401]{1,0,2:T(2,128)}, u32[]{:S(2)}) copy-start(f32[2,128,401]{1,0,2:T(2,128)} %param.34) | copy-start | bytes 1231876
  164.5 70.7 %copy-start.11 = (f32[2,128,401]{1,0,2:T(2,128)S(1)}, f32[2,128,401]{1,0,2:T(2,128)}, u32[]{:S(2)}) copy-start(f32[2,128,401]{1,0,2:T(2,128)} %param.35) | copy-start | bytes 1231876
  164.5 124.5 %all-gather.9.cloned.1.call-start = ((), (), s32[]{:S(2)}) async-start(), calls=%async_computation.6 | async-start | bytes 4915200 | tf_op jit(solution)/shard_map/all_gather | solution.py:567
  165.1 70.3 %copy-start.19 = (u32[32]{0:T(128)S(1)}, u32[32]{0:T(128)}, u32[]{:S(2)}) copy-start(u32[32]{0:T(128)} %constant.151) | copy-start | bytes 388
  165.1 261.2 %reduce-scatter.7.cloned.1.call-start = ((), (), s32[]{:S(2)}) async-start(), calls=%async_computation.8 | async-start | bytes 1310720 | tf_op jit(solution)/shard_map/reduce_scatter | solution.py:599
  233.5 238.9 %reduce-scatter.11.cloned.1.call-start = ((), (), s32[]{:S(2)}) async-start(), calls=%async_computation.11 | async-start | bytes 655360 | tf_op jit(solution)/shard_map/reduce_scatter | solution.py:599
  289.0 202.7 %all-gather.11.cloned.1.call-start = ((), (), s32[]{:S(2)}) async-start(), calls=%async_computation.9 | async-start | bytes 1310720 | tf_op jit(solution)/shard_map/all_gather | solution.py:600
  289.0 2.1 copy-start.4
  380.6 3.7 copy-start
  488.7 2.9 copy-start.6
Sparse Core Ops, SparseCore 0:
  11.4 30.5 all-gather.6
  44.5 36.7 all-gather.4
  161.8 71.6 reduce-scatter.4
  237.6 51.2 reduce-scatter.8
  291.1 27.1 reduce-scatter.6
  320.4 20.2 reduce-scatter.10
Sparse Core Ops, SparseCore 1:
  167.1 76.6 all-gather.8
  426.4 27.7 all-gather.10

commit v3 on v2

v3 whole, which is shorter than its diff:
```python
from functools import partial

import jax
import jax.numpy as jnp
from jax import lax
from jax.experimental import pallas as pl
from jax.experimental.pallas import tpu as pltpu
from jax.sharding import PartitionSpec as P

CLASSES = 81
STEP = 5
BETA_ONE = 0.5
BETA_TWO = 0.5
RATE = 0.02
DECAY = 0.01
EPSILON = 1e-08
BINS = 7
CHUNK = 8
STATIC = 5
WINDOW = 24
MORE = 4
SPANS = 17
LANES = 128
MIB = 2**20


def tent(where, cells):
    return 0.5 * sum(jnp.maximum(0.0, 1.0 - jnp.abs(w - cells)) for w in where)


def pool_kernel(channels, side, groups, copies, pick_ref, span_ref, feat_ref, table_ref, *refs):
    out_refs = refs[-7 - copies : -7]
    cols, rows, parts = refs[-7:-5], refs[-5:-3], refs[-3:-1]
    line_ref = refs[-1]
    image = pick_ref[0]
    half = LANES // 2
    offsets = (0.25, 0.75)
    cells = lax.broadcasted_iota(jnp.int32, (side, LANES), 0).astype(jnp.float32)
    bins = lax.broadcasted_iota(jnp.int32, (8, LANES), 0).astype(jnp.float32)

    def at(group):
        return (image * groups + group) * SPANS

    def param(group, k):
        return table_ref[group, k : k + 1, :]

    def weights(group, slot):
        top, x_start, x_step = param(group, 2), param(group, 4), param(group, 5)
        for j in range(BINS):
            where = [jnp.clip(x_start + (j + off) * x_step, 0.0, top) for off in offsets]
            weight = tent(where, cells)
            high = weight.astype(jnp.bfloat16)
            low = (weight - high.astype(jnp.float32)).astype(jnp.bfloat16)
            lanes = pl.ds(j * LANES, LANES)
            cols[slot][0:side, lanes] = high
            cols[slot][side : 2 * side, lanes] = high
            cols[slot][2 * side : 3 * side, lanes] = low
            cols[slot][3 * side : 4 * side, lanes] = low

    def fill(group, slot, row):
        y_start, y_step, top, base = (param(group, k) for k in range(4))
        where = [jnp.clip(y_start + (bins + off) * y_step, 0.0, top) for off in offsets]
        for h in range(CHUNK):
            rows[slot][row + h] = tent(where, (row + h).astype(jnp.float32) - base)
        place = pl.ds(pl.multiple_of(row * channels, channels), CHUNK * channels)
        left = feat_ref[place, :]
        left = jnp.concatenate([left, left], axis=1)
        parts[slot][place, :] = jnp.dot(left, cols[slot][...], preferred_element_type=jnp.float32)

    def rest(group, slot):
        first = span_ref[at(group)] + STATIC * CHUNK

        @pl.loop(0, span_ref[at(group) + 1])
        def _(t):
            fill(group, slot, first + t * CHUNK)

    def block(slot, i, low_row, count):
        accs = None
        for h in range(count):
            start = pl.multiple_of((low_row + h) * channels, channels)
            weight = jnp.broadcast_to(rows[slot][low_row + h, i : i + 1, :], (channels, LANES))
            new = [
                weight * parts[slot][pl.ds(start, channels), j * LANES : (j + 1) * LANES] for j in range(BINS)
            ]
            accs = new if accs is None else [x + y for x, y in zip(accs, new)]
        return accs

    def spot(i, j):
        return pl.ds(i * BINS + j, channels, stride=BINS * BINS)

    def work(group, slot, following):
        for i in range(BINS):
            accs = block(slot, i, span_ref[at(group) + 3 + i], WINDOW)
            for j in range(BINS):
                line_ref[slot, spot(i, j), :] = accs[j]
            if i < STATIC:
                fill(following, 1 - slot, span_ref[at(following)] + i * CHUNK)

        @pl.when(span_ref[at(group) + 2] > 0)
        def _():
            for i in range(BINS):
                low_row = span_ref[at(group) + 3 + i] + WINDOW

                @pl.loop(0, span_ref[at(group) + 3 + BINS + i])
                def _(t):
                    more = block(slot, i, low_row + t * MORE, MORE)
                    for j in range(BINS):
                        line_ref[slot, spot(i, j), :] = line_ref[slot, spot(i, j), :] + more[j]

    step = pl.program_id(0)

    @pl.when(step == 0)
    def _():
        weights(0, 0)
        for i in range(STATIC):
            fill(0, 0, span_ref[at(0)] + i * CHUNK)
        rest(0, 0)

    group = 2 * step
    weights(group + 1, 1)
    work(group, 0, group + 1)
    rest(group + 1, 1)
    following = jnp.minimum(group + 2, groups - 1)
    weights(following, 0)
    work(group + 1, 1, following)
    rest(following, 0)
    a, b = line_ref[0], line_ref[1]
    lanes = lax.broadcasted_iota(jnp.int32, a.shape, 1)
    new = [jnp.where(lanes < half, a, pltpu.roll(b, half, 1)), jnp.where(lanes < half, pltpu.roll(a, half, 1), b)]
    for out_ref in out_refs:
        for p in range(2):
            out_ref[p] = new[p].astype(jnp.bfloat16)


def pool(feat, table, spans, source, image, images, channels, buffer=None):
    depth = feat.shape[2]
    groups = table.shape[1]
    wide = channels * BINS * BINS
    side = depth // 2
    rows = sum(side >> k for k in range(4))
    boxes = groups * LANES // 2
    blocks = groups // 2
    pick = jnp.stack([source, image])
    out_shape = [jax.ShapeDtypeStruct((2, wide, images * boxes), jnp.bfloat16)]
    out_specs = [pl.BlockSpec((2, wide, LANES), lambda s, pick, spans: (0, 0, pick[1] * blocks + s))]
    in_specs = [
        pl.BlockSpec((None, rows * channels, depth), lambda s, pick, spans: (pick[0], 0, 0)),
        pl.BlockSpec((None, groups, 8, LANES), lambda s, pick, spans: (pick[0], 0, 0, 0)),
    ]
    operands = (pick, spans, feat, table)
    aliases = {}
    if buffer is None:
        out_shape.append(jax.ShapeDtypeStruct((2, wide, boxes), jnp.bfloat16))
        out_specs.append(pl.BlockSpec((2, wide, LANES), lambda s, pick, spans: (0, 0, s)))
    else:
        in_specs.append(pl.BlockSpec(memory_space=pl.ANY))
        operands += (buffer,)
        aliases = {4: 0}
    return pl.pallas_call(
        partial(pool_kernel, channels, side, groups, len(out_shape)),
        out_shape=out_shape,
        grid_spec=pltpu.PrefetchScalarGridSpec(
            num_scalar_prefetch=2,
            grid=(blocks,),
            in_specs=in_specs,
            out_specs=out_specs,
            scratch_shapes=[
                pltpu.VMEM((4 * side, BINS * LANES), jnp.bfloat16),
                pltpu.VMEM((4 * side, BINS * LANES), jnp.bfloat16),
                pltpu.VMEM((rows, 8, LANES), jnp.float32),
                pltpu.VMEM((rows, 8, LANES), jnp.float32),
                pltpu.VMEM((rows * channels, BINS * LANES), jnp.float32),
                pltpu.VMEM((rows * channels, BINS * LANES), jnp.float32),
                pltpu.VMEM((2, wide, LANES), jnp.float32),
            ],
        ),
        input_output_aliases=aliases,
        compiler_params=pltpu.CompilerParams(vmem_limit_bytes=44 * MIB),
        cost_estimate=pl.CostEstimate(
            flops=groups * 40 * channels * BINS * LANES * 8 * depth,
            bytes_accessed=80 * MIB,
            transcendentals=0,
        ),
        name="pool_rois",
    )(*operands)


def feature_rows(maps):
    side = maps[0].shape[-1]
    parts = [
        jnp.pad(m.transpose(0, 2, 1, 3), ((0, 0), (0, 0), (0, 0), (0, side - m.shape[-1])))
        for m in maps
    ]
    full = jnp.concatenate(parts, axis=1)
    high = lax.reduce_precision(full, 8, 7)
    low = (full - high).astype(jnp.bfloat16)
    full = jnp.concatenate([high.astype(jnp.bfloat16), low], axis=-1)
    return full.reshape(-1, 2 * side)


def box_order(boxes, levels, side):
    base = 2 * side - 2 * (side >> levels)
    key = ((boxes[..., 1] + boxes[..., 3]) >> levels) + base * 8
    key = key * key.shape[-1] + jnp.arange(key.shape[-1], dtype=jnp.int32)
    return jnp.sum((key[..., :, None] > key[..., None, :]).astype(jnp.int32), axis=-1)


def sort_boxes(boxes, levels, rank):
    count = boxes.shape[1]
    hot = (rank[:, None, :] == jnp.arange(count, dtype=jnp.int32)[:, None]).astype(jnp.bfloat16)
    both = jnp.concatenate([boxes, levels[..., None]], axis=-1).astype(jnp.bfloat16)
    return jnp.einsum("psr,prk->kps", hot, both, preferred_element_type=jnp.float32).astype(jnp.bfloat16)


def box_table(boxes, side):
    images, _, _, count = boxes.shape
    x0, y0, x1, y1, level = (boxes[:, k].astype(jnp.float32) for k in range(5))
    rows = sum(side >> k for k in range(4))
    scale = jnp.where(level < 0.5, 0.25, jnp.where(level < 1.5, 0.125, jnp.where(level < 2.5, 0.0625, 0.03125)))
    height = scale * (4 * side)
    base = 2.0 * side - 2.0 * height
    top = height - 1.0

    def axis(low, high):
        return low * scale - 0.5, ((high - low) * scale) / 7.0

    x_start, x_step = axis(x0, x1)
    y_start, y_step = axis(y0, y1)
    half = LANES // 2
    groups = count // half

    def split(v):
        return v.reshape(v.shape[:-1] + (groups, half))

    lows, highs = [], []
    for i in range(BINS):
        low = base + jnp.floor(jnp.clip(y_start + (i + 0.25) * y_step, 0.0, top))
        high = base + jnp.floor(jnp.clip(y_start + (i + 0.75) * y_step, 0.0, top)) + 1.0
        lows.append(jnp.min(split(low), axis=(1, 3)))
        highs.append(jnp.max(split(jnp.minimum(high, rows - 1.0)), axis=(1, 3)))
    low = jnp.stack(lows, axis=-1).astype(jnp.int32)
    high = jnp.stack(highs, axis=-1).astype(jnp.int32)
    least = jnp.min(low, axis=-1)
    chunks = jnp.maximum((jnp.max(high, axis=-1) - least + CHUNK) // CHUNK, STATIC)
    first = jnp.clip(rows - chunks * CHUNK, 0, least)
    extra = jnp.maximum(high - low + MORE - WINDOW, 0) // MORE
    low = jnp.minimum(low, (first + chunks * CHUNK)[..., None] - WINDOW - MORE * extra)
    heads = jnp.stack([first, chunks - STATIC, jnp.max(extra, axis=-1)], axis=-1)
    spans = jnp.concatenate([heads, low, extra], axis=-1).reshape(-1)
    zero = jnp.zeros_like(base)
    table = jnp.stack([split(v) for v in (y_start, y_step, top, base, x_start, x_step, zero, zero)])
    return table.transpose(1, 3, 0, 2, 4).reshape(images, groups, 8, LANES), spans


def adamw(weight, moment, second, grad):
    moment = BETA_ONE * moment + (1.0 - BETA_ONE) * grad
    second = BETA_TWO * second + (1.0 - BETA_TWO) * grad * grad
    fixed_m = moment / (1.0 - BETA_ONE**STEP)
    fixed_v = second / (1.0 - BETA_TWO**STEP)
    weight = weight - RATE * (fixed_m / (jnp.sqrt(fixed_v) + EPSILON) + DECAY * weight)
    return (weight, moment, second)


def update_kernel(pooled_ref, back_ref, w_ref, m_ref, v_ref, *outs):
    grad = jnp.dot(pooled_ref[...], back_ref[...], preferred_element_type=jnp.float32)
    new = adamw(w_ref[...], m_ref[...], v_ref[...], grad)
    for ref, value in zip(outs, new):
        ref[...] = value


def update_first(pooled, back, weight, moment, second):
    passes, wide, hidden = weight.shape
    boxes = pooled.shape[2]
    block = wide // BINS
    big = pl.BlockSpec((None, block, hidden), lambda p, b: (p, b, 0))
    return pl.pallas_call(
        update_kernel,
        out_shape=[jax.ShapeDtypeStruct(weight.shape, jnp.float32)] * 3,
        grid=(passes, BINS),
        in_specs=[
            pl.BlockSpec((None, block, boxes), lambda p, b: (p, b, 0)),
            pl.BlockSpec((None, boxes, hidden), lambda p, b: (p, 0, 0)),
            big,
            big,
            big,
        ],
        out_specs=[big] * 3,
        compiler_params=pltpu.CompilerParams(vmem_limit_bytes=56 * MIB),
        cost_estimate=pl.CostEstimate(
            flops=2 * passes * wide * hidden * boxes,
            bytes_accessed=passes * wide * hidden * 24 + passes * boxes * (wide + hidden) * 2,
            transcendentals=passes * wide * hidden,
        ),
        name="update_first",
    )(pooled, back, weight, moment, second)


def loss_and_slope(logits, box, count):
    place = lax.broadcasted_iota(jnp.int32, logits.shape, 1)
    is_class = place < CLASSES
    label = box[:, 0:1].astype(jnp.int32)
    weight = box[:, 1:2]
    top = jnp.max(jnp.where(is_class, logits, -jnp.inf), axis=1, keepdims=True)
    grown = jnp.where(is_class, jnp.exp(jnp.where(is_class, logits - top, 0.0)), 0.0)
    norm = jnp.sum(grown, axis=1, keepdims=True)
    hot = place == label
    picked = jnp.sum(jnp.where(hot, logits, 0.0), axis=1, keepdims=True)
    fore = jnp.where(label > 0, weight, 0.0)
    rows = weight * (top + jnp.log(norm) - picked)
    slope = weight * (grown / norm - jnp.where(hot, 1.0, 0.0))
    offset = place - (CLASSES + 4 * (label - 1))
    for k in range(4):
        mask = (offset == k) & (place >= CLASSES)
        chosen = jnp.sum(jnp.where(mask, logits, 0.0), axis=1, keepdims=True)
        differ = fore * (chosen - box[:, 2 + k : 3 + k])
        near = jnp.abs(differ)
        rows += jnp.where(near < 1.0, 0.5 * differ * differ, near - 0.5) * fore
        slope = jnp.where(mask, fore * jnp.clip(differ, -1.0, 1.0), slope)
    return rows, slope / count


def sigmoid(value):
    return 1.0 / (1.0 + jnp.exp(-value))


def head_kernel(
    images, parts, mine,
    part_ref, weight_ref, box_ref, count_ref,
    back_ref, kept_ref,
    sums, landed, own, rs_send, rs_recv, ag_send, ag_recv, up_send, up_recv, down_send, down_recv, own_sem,
):
    me = lax.axis_index("narrow")
    level = lax.axis_index("wide")
    bits = parts.bit_length() - 1
    turn = [(1 - 2 * ((me // 2**k) % 2)) * 2**k for k in range(bits)]

    def peer(mask):
        return me + sum((turn[k] for k in range(bits) if mask >> k & 1), 0)

    links = list(range(1, bits))
    orders = [links, links[::-1]]

    barrier = pltpu.get_barrier_semaphore()
    for k in range(bits):
        pl.semaphore_signal(barrier, inc=1, device_id={"narrow": peer(1 << k)})

    @pl.when(level > 0)
    def _():
        pl.semaphore_signal(barrier, inc=1, device_id={"wide": level - 1})

    @pl.when(level < images - 1)
    def _():
        pl.semaphore_signal(barrier, inc=1, device_id={"wide": level + 1})

    ends = jnp.where(level > 0, 1, 0) + jnp.where(level < images - 1, 1, 0)
    pl.semaphore_wait(barrier, bits + ends)

    def scatter(p, mask, bit, source):
        return pltpu.make_async_remote_copy(
            src_ref=source,
            dst_ref=landed.at[p, mask],
            send_sem=rs_send.at[p, mask],
            recv_sem=rs_recv.at[p, mask],
            device_id={"narrow": peer(1 << bit)},
        )

    def part_at(p, mask):
        return part_ref.at[p, pl.ds(pl.multiple_of(peer(mask) * mine, mine), mine), :]

    copies = {}
    for p in range(2):
        for mask in range(1, parts, 2):
            copies[p, mask] = scatter(p, mask, 0, part_at(p, mask))
            copies[p, mask].start()

    def stage(p, at):
        order = [0] + orders[p]
        bit = order[at - 1]
        seen = sum(1 << b for b in order[:at])
        for mask in range(parts):
            if mask & seen:
                continue
            copies[p, mask | 1 << bit].wait_recv()
            if at == 1:
                have = part_ref[p, pl.ds(pl.multiple_of(peer(mask) * mine, mine), mine), :]
            else:
                have = sums[p, mask]
            sums[p, mask] = have + landed[p, mask | 1 << bit]
            if at < bits and mask >> order[at] & 1:
                copies[p, mask] = scatter(p, mask, order[at], sums.at[p, mask])
                copies[p, mask].start()

    for at in range(1, bits):
        for p in range(2):
            stage(p, at)

    def rows(p, image, mask):
        place = (image * parts + peer(mask)) * mine
        return back_ref.at[p, pl.ds(pl.multiple_of(place, mine), mine), :]

    def spread(p, image, mask, bit, source=None):
        spot = rows(p, image, mask)
        there = mask | 1 << bit
        return pltpu.make_async_remote_copy(
            src_ref=spot if source is None else source,
            dst_ref=spot,
            send_sem=ag_send.at[p, image, there],
            recv_sem=ag_recv.at[p, image, there],
            device_id={"narrow": peer(1 << bit)},
        )

    def arrive(p, image, mask):
        spot = rows(p, image, mask)
        pltpu.make_async_remote_copy(
            src_ref=spot, dst_ref=spot, send_sem=ag_send.at[p, image, mask],
            recv_sem=ag_recv.at[p, image, mask], device_id={"narrow": peer(1)},
        ).wait_recv()

    def hop(p, d, up, source=None):
        image = level - d if up else level + d
        spot = rows(p, image, 0)
        return pltpu.make_async_remote_copy(
            src_ref=spot if source is None else source,
            dst_ref=spot,
            send_sem=(up_send if up else down_send).at[p, d],
            recv_sem=(up_recv if up else down_recv).at[p, d],
            device_id={"wide": level + 1 if up else level - 1},
        )

    def came(p, d, up):
        image = level - d if up else level + d
        spot = rows(p, image, 0)
        pltpu.make_async_remote_copy(
            src_ref=spot, dst_ref=spot, send_sem=(up_send if up else down_send).at[p, d],
            recv_sem=(up_recv if up else down_recv).at[p, d - 1],
            device_id={"wide": level - 1 if up else level + 1},
        ).wait_recv()

    steps = [orders[p] + [0] for p in range(2)]

    def masks_before(p, at):
        seen = sum(1 << b for b in steps[p][:at])
        return [m for m in range(parts) if not m & ~seen]

    def advance(p, image, at, source=None):
        bit = steps[p][at]
        if at:
            last = steps[p][at - 1]
            for m in masks_before(p, at - 1):
                arrive(p, image, m | 1 << last)
        for m in masks_before(p, at):
            spread(p, image, m, bit, source if m == 0 else None).start()

    def finish(p, image):
        last = steps[p][-1]
        for m in masks_before(p, bits - 1):
            arrive(p, image, m | 1 << last)
        for at in range(bits):
            for m in masks_before(p, at):
                spread(p, image, m, steps[p][at]).wait_send()

    count = count_ref[0:1, 0:1]
    hidden = part_ref.shape[2]
    for p in range(2):
        stage(p, bits)
        pre1 = sums[p, 0]
        sig1 = sigmoid(pre1)
        hid1 = (pre1 * sig1).astype(jnp.bfloat16)
        pre2 = jnp.dot(hid1, weight_ref[p, :, :hidden], preferred_element_type=jnp.float32)
        sig2 = sigmoid(pre2)
        hid2 = (pre2 * sig2).astype(jnp.bfloat16)
        logits = jnp.dot(hid2, weight_ref[p, :, hidden:], preferred_element_type=jnp.float32)
        loss, slope = loss_and_slope(logits, box_ref[p], count)
        back_z = slope.astype(jnp.bfloat16)
        turned = (((1,), (1,)), ((), ()))
        back_h2 = lax.dot_general(back_z, weight_ref[p, :, hidden:], turned, preferred_element_type=jnp.float32)
        back_p2 = (back_h2 * (sig2 * (1.0 + pre2 * (1.0 - sig2)))).astype(jnp.bfloat16)
        back_h1 = lax.dot_general(back_p2, weight_ref[p, :, :hidden], turned, preferred_element_type=jnp.float32)
        own[p] = (back_h1 * (sig1 * (1.0 + pre1 * (1.0 - sig1)))).astype(jnp.bfloat16)

        @pl.when(level < images - 1)
        def _():
            hop(p, 0, True, own.at[p]).start()

        @pl.when(level > 0)
        def _():
            hop(p, 0, False, own.at[p]).start()

        advance(p, level, 0, own.at[p])
        pltpu.make_async_copy(own.at[p], rows(p, level, 0), own_sem.at[p]).start()
        place = lax.broadcasted_iota(jnp.int32, (mine, LANES), 1)
        losses = jnp.zeros((mine, LANES), jnp.float32)
        for k in range(3):
            near = loss.astype(jnp.bfloat16).astype(jnp.float32)
            losses = jnp.where(place == k, near, losses)
            loss = loss - near
        at = 0
        for value in (hid1, hid2, back_p2, back_z, losses.astype(jnp.bfloat16)):
            kept_ref[p, :, at : at + value.shape[1]] = value
            at += value.shape[1]
    for p in range(2):
        pltpu.make_async_copy(own.at[p], rows(p, level, 0), own_sem.at[p]).wait()

    def each_side(d, do):
        @pl.when(level >= d)
        def _():
            do(level - d, True)

        @pl.when(level + d < images)
        def _():
            do(level + d, False)

    def enter(d):
        def do(image, up):
            for p in range(2):
                came(p, d, up)

                @pl.when((level < images - 1) if up else (level > 0))
                def _():
                    hop(p, d, up).start()

                advance(p, image, 0)

        each_side(d, do)

    def go_on(d, at):
        if d == 0:
            for p in range(2):
                advance(p, level, at)
        else:

            def do(image, up):
                for p in range(2):
                    advance(p, image, at)

            each_side(d, do)

    for tick in range(1, images + bits - 1):
        for d in range(images):
            at = tick - d
            if at == 0:
                enter(d)
            elif 0 < at < bits:
                go_on(d, at)

    for p in range(2):
        finish(p, level)

        @pl.when(level < images - 1)
        def _():
            hop(p, 0, True).wait_send()

        @pl.when(level > 0)
        def _():
            hop(p, 0, False).wait_send()

    for d in range(1, images):

        def do(image, up):
            for p in range(2):
                finish(p, image)

                @pl.when((level < images - 1) if up else (level > 0))
                def _():
                    hop(p, d, up).wait_send()

        each_side(d, do)
    for p in range(2):
        for mask in range(1, parts):
            copies[p, mask].wait_send()


def head_step(part, weight, box, count, images, parts):
    passes, boxes, hidden = part.shape
    mine = boxes // parts
    outs = weight.shape[2] - hidden
    low = jnp.bfloat16
    vmem = pl.BlockSpec(memory_space=pltpu.VMEM)
    dma = pltpu.SemaphoreType.DMA
    return pl.pallas_call(
        partial(head_kernel, images, parts, mine),
        out_shape=[
            jax.ShapeDtypeStruct((passes, images * boxes, hidden), low),
            jax.ShapeDtypeStruct((passes, mine, 3 * hidden + outs + LANES), low),
        ],
        in_specs=[vmem] * 4,
        out_specs=[pl.BlockSpec(memory_space=pl.ANY), vmem],
        scratch_shapes=[
            pltpu.VMEM((passes, parts, mine, hidden), jnp.float32),
            pltpu.VMEM((passes, parts, mine, hidden), jnp.float32),
            pltpu.VMEM((passes, mine, hidden), low),
            dma((passes, parts)),
            dma((passes, parts)),
            dma((passes, images, parts)),
            dma((passes, images, parts)),
            dma((passes, images)),
            dma((passes, images)),
            dma((passes, images)),
            dma((passes, images)),
            dma((passes,)),
        ],
        compiler_params=pltpu.CompilerParams(
            vmem_limit_bytes=48 * MIB, collective_id=0, has_side_effects=True
        ),
        cost_estimate=pl.CostEstimate(
            flops=8 * passes * mine * hidden * (hidden + outs),
            bytes_accessed=100 * MIB,
            transcendentals=4 * passes * mine * hidden,
        ),
        name="head_step",
    )(part, weight, box, count)


def own_gradient(kept, hidden, outs):
    parts = lax.axis_size("narrow")
    span = hidden // parts
    at = lax.axis_index("narrow") * span
    end = kept.shape[2] - LANES

    def rows(start):
        return lax.dynamic_slice_in_dim(kept, start + at, span, 2)

    def by(left, right):
        return lax.dot_general(left, right, (((1,), (1,)), ((0,), (0,))), preferred_element_type=jnp.float32)

    two = by(rows(0), kept[..., 2 * hidden : 3 * hidden])
    head = by(rows(hidden), kept[..., 3 * hidden : end])
    loss = jnp.sum(kept[..., end : end + 3].astype(jnp.float32))
    grad = jnp.concatenate([two, head], axis=2)
    spot = [lax.broadcasted_iota(jnp.int32, grad.shape, k) for k in range(3)]
    spot = (spot[0] == 0) & (spot[1] == 0) & (spot[2] == grad.shape[2] - 1)
    return jnp.where(spot, loss, grad)


def per_device(
    feat_p2, feat_p3, feat_p4, feat_p5, rois, levels, labels, sampled, targets,
    fc1_w, fc1_m, fc1_v, fc2_w, fc2_m, fc2_v, head_w, head_m, head_v,
):
    side = feat_p2.shape[-1]
    channels = feat_p2.shape[1]
    boxes = rois.shape[2]
    images = lax.axis_size("wide")
    mine = boxes // lax.axis_size("narrow")
    first = lax.axis_index("narrow") * mine
    level = lax.axis_index("wide").astype(jnp.int32)
    parts = lax.axis_size("narrow")
    hidden = fc2_w.shape[2]
    outs = head_w.shape[2]
    zero = jnp.zeros((), jnp.int32)
    rank = box_order(rois[:, 0], levels[:, 0], side)
    ordered = sort_boxes(rois[:, 0], levels[:, 0], rank)
    feat = feature_rows((feat_p2, feat_p3, feat_p4, feat_p5))
    height = feat.shape[0]
    flags = sampled[:, 0].astype(jnp.bfloat16).reshape(1, 2, boxes)
    tail = jnp.concatenate([ordered, flags]).reshape(-1, LANES)
    weight = jnp.concatenate([fc2_w, jnp.pad(head_w, ((0, 0), (0, 0), (0, -outs % LANES)))], axis=2)
    weight = lax.all_gather(weight.astype(jnp.bfloat16), "narrow", axis=1, tiled=True)
    feats = lax.all_gather(jnp.concatenate([feat, tail]), "wide", axis=0)
    tails = feats[:, height:].reshape(images, 6, 2, boxes)
    count = jnp.sum(tails[:, 5].astype(jnp.float32))

    table, spans = box_table(ordered[None], side)
    pooled, own = pool(feat[None], table, spans, zero, level, images, channels)
    w1 = fc1_w.astype(jnp.bfloat16)
    part = lax.dot_general(own, w1, (((1,), (1,)), ((0,), (0,))), preferred_element_type=jnp.float32)
    hot = rank[:, None, :] == first + jnp.arange(mine, dtype=jnp.int32)[:, None]

    def pick(values):
        return jnp.sum(jnp.where(hot, values[:, 0].astype(jnp.float32)[:, None, :], 0), axis=-1)

    box = [pick(labels), pick(sampled)] + [pick(targets[..., k]) for k in range(4)]
    box = jnp.pad(jnp.stack(box, axis=-1), ((0, 0), (0, 0), (0, LANES - 6)))
    back, kept = head_step(part, weight, box, jnp.full((8, LANES), count), images, parts)

    tables, all_spans = box_table(tails[:, :5], side)
    kept = lax.all_gather(kept, "narrow", axis=1, tiled=True)
    turn = [lax.rem(level + k, images) for k in range(1, images)]
    held = max(images - 2, 1)
    for k in range(images - 1):
        if k == held:
            kept, pooled = lax.optimization_barrier((kept, pooled))
            grad = own_gradient(kept, hidden, outs)
            grad, pooled = lax.optimization_barrier((grad, pooled))
            grad = lax.psum_scatter(grad, "wide", scatter_dimension=1, tiled=True)
        pooled = pool(feats, tables, all_spans, turn[k], turn[k], images, channels, pooled)[0]
    grad, pooled = lax.optimization_barrier((grad, pooled))
    grad = lax.all_gather(grad, "wide", axis=1, tiled=True)
    new1 = update_first(pooled, back, fc1_w, fc1_m, fc1_v)
    grad, new1 = lax.optimization_barrier((grad, new1))
    total = grad[0, 0, -1]
    new2 = adamw(fc2_w, fc2_m, fc2_v, grad[..., :hidden])
    newh = adamw(head_w, head_m, head_v, grad[..., hidden : hidden + outs])
    return (jnp.stack([total, count]),) + tuple(new1) + tuple(new2) + tuple(newh)


def solution(mesh):
    maps = P("wide", "narrow", None, None)
    rows = P(None, "narrow", None)
    box = P(None, "wide", None)
    coords = P(None, "wide", None, None)
    return jax.shard_map(
        per_device,
        mesh=mesh,
        in_specs=(maps,) * 4 + (coords, box, box, box, coords) + (rows,) * 9,
        out_specs=(P(),) + (rows,) * 9,
        check_vma=False,
    )
```

time: 504 us -> 383 us (0.76)
  blocking collectives: 70.5 us -> 0 us
  Pallas kernels: 238 us -> 204 us
  waiting for transfers between devices: 126 us -> 94.8 us
  other arithmetic: 13.6 us -> 29.1 us
  matrix products: 18.8 us -> 9.98 us
  local copies, waits for them, and re-layouts: 19.3 us -> 25.8 us
    reduce_scatter x4 -> x1, waiting for transfers between devices: 119 us -> 11.6 us  [per_device(): grad = lax.psum_scatter(grad, 'wide', scatter_dimension=1, tiled=True)]
    all_gather x4, waiting for transfers between devices: 5.69 us -> 83.2 us  [the longest x1 45.1 us: per_device(): lax.all_gather(weight.astype(jnp.bfloat16), 'narrow', axis=1, tiled=True)]
    unnamed x1 -> x0, blocking collectives: 39.4 us -> none
    pallas_call x3 -> x5, Pallas kernels: 165 us -> 130 us  [the longest x4 89.5 us: pool(): pl.pallas_call(partial(pool_kernel, channels, side, groups, len(out_shape...]
    all_gather x2 -> x0, blocking collectives: 31.1 us -> none  [the longest x1 16 us: over_all(): return lax.all_gather(grad, 'wide', axis=1, tiled=True)]
    dot_general x1, matrix products: 10.9 us -> 5.67 us  [per_device(): lax.dot_general(own, w1, (((1,), (1,)), ((0,), (0,))), preferred_element_...]
    unnamed x63 -> x70, local copies, waits for them, and re-layouts: 15.5 us -> 15.2 us
  transfers between devices with their start and end apart: 8 -> 5, of which waited for: 3 -> 4; matrix products, arithmetic and copies ran while one was open for 6% -> 7% of each run, Pallas kernels for 33% -> 34%
where the time goes in v3:
time: 383 us; the launch traced here: 379 us
  Pallas kernels  204 us (53%)
  waiting for transfers between devices  94.8 us (25%)
  other arithmetic  29.1 us (8%)
  local copies, waits for them, and re-layouts  25.8 us (7%)
  between operations  14.6 us (4%)
  matrix products  9.98 us (3%)
    pallas_call x4, Pallas kernels, pool(): pl.pallas_call(partial(pool_kernel, channels, side, groups, len(out_shape...  89.5 us
    pallas_call x1, Pallas kernels, head_step(): pl.pallas_call(partial(head_kernel, images, parts, mine), out_shape=[jax....  73.7 us
    all_gather x1, waiting for transfers between devices, per_device(): lax.all_gather(weight.astype(jnp.bfloat16), 'narrow', axis=1, tiled=True)  45.1 us
    pallas_call x1, Pallas kernels, update_first(): pl.pallas_call(update_kernel, out_shape=[jax.ShapeDtypeStruct(weight.shap...  40.6 us
    all_gather x1, waiting for transfers between devices, per_device(): feats = lax.all_gather(jnp.concatenate([feat, tail]), 'wide', axis=0)  37.9 us
    unnamed x70, local copies, waits for them, and re-layouts  15.2 us
    reduce_scatter x1, waiting for transfers between devices, per_device(): grad = lax.psum_scatter(grad, 'wide', scatter_dimension=1, tiled=True)  11.6 us
  transfers between devices with their start and end apart: 5, of which 4 were waited for; matrix products, arithmetic and copies ran while one was open for 7% of the time, Pallas kernels for 34%

profile of v3, /device:TPU:0, one launch (start us, length us, event | category | flops | bytes accessed | tf_op | source)
XLA Modules:
  0.0 378.5 jit_solution(1545710641040025796)
XLA Ops:
  7.2 0.9 bitcast_convert_fusion
  8.1 0.8 fusion.36
  8.9 0.7 bitcast_convert_fusion.1
  9.6 0.4 convert_reduce_fusion
  10.0 0.5 fusion.10
  10.5 1.4 fusion.57
  11.9 1.1 copy.272
  13.0 0.9 copy.273
  13.9 1.2 select_maximum_fusion
  15.1 0.4 copy.218
  15.5 0.3 reduce-precision_convert_fusion
  15.8 1.5 pad_maximum_fusion
  17.5 1.8 convert.25
  19.3 1.8 copy.225
  21.1 1.9 fusion.15
  23.0 0.2 all-gather.8.cloned.1.call-start
  23.2 0.1 minimum_reduce_fusion.7
  23.8 0.1 reduce_min.211
  24.0 0.1 reduce_min.217
  24.2 0.1 reduce_min.187
  24.4 0.1 reduce_min.190
  24.6 0.1 reduce_min.196
  25.2 0.1 reduce_max.212
  25.4 0.1 reduce_max.218
  25.6 0.1 reduce_max.224
  25.8 0.1 reduce_max.227
  27.5 0.7 convert_element_type.570
  28.2 0.9 fusion.56
  29.1 0.7 copy_bitcast_fusion.4
  29.8 0.3 fusion.22
  30.4 0.3 reduce-precision_convert_fusion.1
  30.7 0.5 pad_maximum_fusion.1.feat_ref
  31.3 22.6 %pool_rois.4 = (bf16[2,1568,2048]{2,1,0:T(8,128)(2,1)}, bf16[2,1568,512]{2,1,0:T(8,128)(2,1)S(1)}) custom-call(s32[2]{0:T(128)S(1)} %pad_add_fusion.pick_ref, s32[136]{0:T(256)S(1)} %reshape.1644.span_ref, bf16[1,3840,128]{2,1,0:T(8,128)(2,1)S(1)} %pad_maximum_fusion.1.feat_ref, f32[1,8,8,128]{3,2,1,0:T(8,128)S(1)} %reshape.1645.table_ref), custom_call_target="tpu_custom_call" | custom-call | flops 9395240960 | bytes 83886080 | tf_op jit(solution)/shard_map/pool_rois/pallas_call | solution.py:159
  53.9 5.7 %fusion.part_ref = f32[2,512,1024]{2,1,0:T(8,128)} fusion(bf16[2,1568,512]{2,1,0:T(8,128)(2,1)S(1)} %get-tuple-element.27, f32[2,1568,1024]{2,1,0:T(8,128)S(1)} %bitcast.196), kind=kOutput, calls=%fused_computation | convolution fusion | flops 3291545600 | bytes 20250624 | tf_op jit(solution)/shard_map/dot_general | solution.py:665
  59.6 37.9 %all-gather.12.cloned.1.call-done = bf16[15552,128]{1,0:T(8,128)(2,1)} async-done(((bf16[3888,128]{1,0:T(8,128)(2,1)}), bf16[15552,128]{1,0:T(8,128)(2,1)}) %all-gather.12.cloned.1.call-update) | async-done | bytes 3981328 | tf_op jit(solution)/shard_map/all_gather | solution.py:658
  97.6 0.8 slice.109
  98.4 0.6 convert_reduce_fusion.2
  99.0 45.1 %all-gather.6.cloned.1.call-done.weight_ref = bf16[2,1024,1536]{2,1,0:T(8,128)(2,1)} async-done(((bf16[2,128,1536]{2,1,0:T(8,128)(2,1)}), bf16[2,1024,1536]{2,1,0:T(8,128)(2,1)}) %all-gather.6.cloned.1.call-update) | async-done | bytes 6291472 | tf_op jit(solution)/shard_map/all_gather | solution.py:657
  144.2 0.6 broadcast_in_dim.128.count_ref
  144.8 2.2 copy-done
  147.0 73.7 %head_step.1 = (bf16[2,2048,1024]{2,1,0:T(8,128)(2,1)}, bf16[2,64,3712]{2,1,0:T(8,128)(2,1)}) custom-call(f32[2,512,1024]{2,1,0:T(8,128)S(1)} %copy-done, bf16[2,1024,1536]{2,1,0:T(8,128)(2,1)} %all-gather.6.cloned.1.call-done.weight_ref, f32[2,64,128]{2,1,0:T(8,128)S(1)} %pad.25.box_ref, f32[8,128]{1,0:T(8,128)S(1)} %broadcast_in_dim.128.count_ref), custom_call_target="tpu_custom_call" | custom-call | flops 1610612736 | bytes 104857600 | tf_op jit(solution)/shard_map/head_step/pallas_call | solution.py:580
  221.1 0.2 minimum_reduce_fusion
  224.7 0.2 reshape.1649.table_ref
  225.5 2.1 copy-done.1
  227.7 22.1 %pool_rois.5.refs_0_ = bf16[2,1568,2048]{2,1,0:T(8,128)(2,1)} custom-call(s32[2]{0:T(128)S(1)} %pad_add_fusion.2.pick_ref, s32[544]{0:T(1024)S(1)} %reshape.1648.span_ref, bf16[4,3888,128]{2,1,0:T(8,128)(2,1)S(1)} %bitcast.192, f32[4,8,8,128]{3,2,1,0:T(8,128)S(1)} %reshape.1649.table_ref, ...), custom_call_target="tpu_custom_call", output_to_operand_aliasing={{}: (4, {})} | custom-call | flops 9395240960 | bytes 83886080 | tf_op jit(solution)/shard_map/pool_rois/pallas_call | solution.py:159
  249.8 22.5 %pool_rois.6.refs_0_ = bf16[2,1568,2048]{2,1,0:T(8,128)(2,1)} custom-call(s32[2]{0:T(128)S(1)} %pad_add_fusion.1.pick_ref, s32[544]{0:T(1024)S(1)} %reshape.1648.span_ref, bf16[4,3888,128]{2,1,0:T(8,128)(2,1)S(1)} %bitcast.193, f32[4,8,8,128]{3,2,1,0:T(8,128)S(1)} %reshape.1649.table_ref, ...), custom_call_target="tpu_custom_call", output_to_operand_aliasing={{}: (4, {})} | custom-call | flops 9395240960 | bytes 83886080 | tf_op jit(solution)/shard_map/pool_rois/pallas_call | solution.py:159
  272.4 1.7 convert_reduce_fusion.1
  274.1 2.2 fusion.2
  276.2 1.7 fusion.12
  277.9 2.0 maximum_select_fusion
  280.1 2.1 copy-done.2
  282.2 22.2 %pool_rois.7.pooled_ref = bf16[2,1568,2048]{2,1,0:T(8,128)(2,1)} custom-call(s32[2]{0:T(128)S(1)} %pad_add_fusion.3.pick_ref, s32[544]{0:T(1024)S(1)} %reshape.1648.span_ref, bf16[4,3888,128]{2,1,0:T(8,128)(2,1)S(1)} %bitcast.194, f32[4,8,8,128]{3,2,1,0:T(8,128)S(1)} %reshape.1649.table_ref, ...), custom_call_target="tpu_custom_call", output_to_operand_aliasing={{}: (4, {})} | custom-call | flops 9395240960 | bytes 83886080 | tf_op jit(solution)/shard_map/pool_rois/pallas_call | solution.py:159
  304.5 11.6 %reduce-scatter.2.cloned.1.call-done = f32[2,32,1536]{2,1,0:T(8,128)} async-done(((f32[2,128,1536]{2,1,0:T(8,128)}), f32[2,32,1536]{2,1,0:T(8,128)}) %reduce-scatter.2.cloned.1.call-update) | async-done | bytes 393232 | tf_op jit(solution)/shard_map/reduce_scatter | solution.py:684
  316.1 0.2 copy.252
  316.3 0.2 copy.249
  316.6 0.2 copy.250
  316.8 40.6 %update_first.1 = (f32[2,1568,1024]{2,1,0:T(8,128)}, f32[2,1568,1024]{2,1,0:T(8,128)}, f32[2,1568,1024]{2,1,0:T(8,128)}) custom-call(bf16[2,1568,2048]{2,1,0:T(8,128)(2,1)} %pool_rois.7.pooled_ref, bf16[2,2048,1024]{2,1,0:T(8,128)(2,1)} %get-tuple-element.36.back_ref, f32[2,1568,1024]{2,1,0:T(8,128)} %w_ref.1, f32[2,1568,1024]{2,1,0:T(8,128)} %m_ref.1, ...), custom_call_target="tpu_custom_call" | custom-call | flops 13153337344 | bytes 98304000 | tf_op jit(solution)/shard_map/update_first/pallas_call | solution.py:276
  357.4 1.3 slice.99
  358.7 2.4 multiply_subtract_fusion.1
  361.1 2.1 copy.253
  363.2 2.0 copy.254
  365.2 1.0 copy.255
  366.1 3.8 %multiply_subtract_fusion = (f32[2,128,1024]{2,1,0:T(8,128)}, f32[2,128,1024]{2,1,0:T(8,128)}, f32[2,128,1024]{2,1,0:T(8,128)}) fusion(f32[2,128,1024]{2,1,0:T(8,128)S(1)} %copy-done.3, f32[2,128,1536]{2,1,0:T(8,128)S(1)} %copy-done.5, f32[2,128,1024]{2,1,0:T(8,128)} %param.31, f32[2,128,1024]{2,1,0:T(8,128)} %param.32), kind=kLoop, calls=%fused_computation.30 | loop fusion | flops 3670016 | bytes 7340032 | tf_op jit(solution)/shard_map/sub | solution.py:260
  369.9 1.9 pad_maximum_fusion.3
  (182 shorter events, 8.0 us)
Async XLA Ops:
  7.2 6.7 %copy-start.6 = (f32[1,32,64,64]{3,2,1,0:T(8,128)S(1)}, f32[1,32,64,64]{3,2,1,0:T(8,128)}, u32[]{:S(2)}) copy-start(f32[1,32,64,64]{3,2,1,0:T(8,128)} %param.18) | copy-start | bytes 1572868
  7.2 90.4 %all-gather.12.cloned.1.call-start = ((), (), s32[]{:S(2)}) async-start(), calls=%async_computation.5 | async-start | bytes 4976640 | tf_op jit(solution)/shard_map/all_gather | solution.py:658
  15.8 1.6 copy-start.3
  17.3 126.9 %all-gather.6.cloned.1.call-start = ((), (), s32[]{:S(2)}) async-start(), calls=%async_computation.1 | async-start | bytes 7077888 | tf_op jit(solution)/shard_map/all_gather | solution.py:657
  23.0 249.4 %all-gather.8.cloned.1.call-start = ((), (), s32[]{:S(2)}) async-start(), calls=%async_computation.2 | async-start | bytes 8552448 | tf_op jit(solution)/shard_map/all_gather | solution.py:676
  30.7 23.2 %slice-start = ((s8[12845056]{0:T(1024)(128)(4,1)}), s8[4194304]{0:T(1024)(128)(4,1)S(1)}, s32[]{:S(2)}) async-start(s8[12845056]{0:T(1024)(128)(4,1)} %bitcast.195), calls=%async_computation.6 | async-start | bytes 8388608
  31.2 22.7 %slice-start.1 = ((s8[12845056]{0:T(1024)(128)(4,1)}), s8[4194304]{0:T(1024)(128)(4,1)S(1)}, s32[]{:S(2)}) async-start(s8[12845056]{0:T(1024)(128)(4,1)} %bitcast.195), calls=%async_computation.7 | async-start | bytes 8388608
  31.3 22.7 %slice-start.2 = ((s8[12845056]{0:T(1024)(128)(4,1)}), s8[4194304]{0:T(1024)(128)(4,1)S(1)}, s32[]{:S(2)}) async-start(s8[12845056]{0:T(1024)(128)(4,1)} %bitcast.195), calls=%async_computation.8 | async-start | bytes 8388608
  31.3 22.7 %slice-start.3 = ((s8[12845056]{0:T(1024)(128)(4,1)}), s8[262144]{0:T(1024)(128)(4,1)S(1)}, s32[]{:S(2)}) async-start(s8[12845056]{0:T(1024)(128)(4,1)} %bitcast.195), calls=%async_computation.9 | async-start | bytes 524288
  144.8 2.2 copy-start
  220.8 95.3 %reduce-scatter.2.cloned.1.call-start = ((), (), s32[]{:S(2)}) async-start(), calls=%async_computation.3 | async-start | bytes 1966080 | tf_op jit(solution)/shard_map/reduce_scatter | solution.py:684
  225.5 2.1 copy-start.1
  280.0 77.4 %all-gather.10.cloned.1.call-start = ((), (), s32[]{:S(2)}) async-start(), calls=%async_computation.4 | async-start | bytes 1966080 | tf_op jit(solution)/shard_map/all_gather | solution.py:687
  280.1 2.1 copy-start.2
  282.2 33.9 %copy-start.4 = (f32[2,128,401]{1,0,2:T(2,128)S(1)}, f32[2,128,401]{1,0,2:T(2,128)}, u32[]{:S(2)}) copy-start(f32[2,128,401]{1,0,2:T(2,128)} %param.33) | copy-start | bytes 1231876
  282.2 34.1 %copy-start.7 = (f32[2,128,401]{1,0,2:T(2,128)S(1)}, f32[2,128,401]{1,0,2:T(2,128)}, u32[]{:S(2)}) copy-start(f32[2,128,401]{1,0,2:T(2,128)} %param.34) | copy-start | bytes 1231876
  304.5 12.1 %copy-start.8 = (f32[2,128,401]{1,0,2:T(2,128)S(1)}, f32[2,128,401]{1,0,2:T(2,128)}, u32[]{:S(2)}) copy-start(f32[2,128,401]{1,0,2:T(2,128)} %param.35) | copy-start | bytes 1231876
  361.1 5.1 %copy-start.5 = (f32[2,128,1536]{2,1,0:T(8,128)S(1)}, f32[2,128,1536]{2,1,0:T(8,128)}, u32[]{:S(2)}) copy-start(f32[2,128,1536]{2,1,0:T(8,128)} %all-gather.10.cloned.1.call-done) | copy-start | bytes 4718596
Sparse Core Ops, SparseCore 0:
  17.4 80.0 all-gather.11
  100.0 44.1 all-gather.5
  220.9 51.4 all-gather.7
  280.1 35.9 reduce-scatter.1
  317.5 36.0 all-gather.9
